TPU v7x, 32 devices: a whole 2x2x4 slice. The times are simulated.
32 devices in a mesh: band: 4 (over x, core), dx: 2 (over y), dyz: 4 (over z).
Axes of the slice: x: 2, y: 2, z: 4, core: 2. Of those that a mesh axis runs over, the one named last changes fastest.
Arguments:
- density: float32 [64, 96, 512], P('dx', 'dyz', 'band'), may hold values from 0.1 to 3
- hartree: float32 [64, 96, 512], P('dx', 'dyz', 'band'), may hold values from -6 to 6
- box_root: int32 [3, 512], P(None, ('dx', 'dyz')), may hold values from 0 to 511, as said below
- species: int32 [512], P(('dx', 'dyz')), may hold values from 0 to 1
- atom_count: int32 [8], P(('dx', 'dyz')), may hold values from 1 to 64, 256 in all
- shape_functions: float32 [2, 25, 4096], replicated, may hold values from -28 to 28
- coupling: float32 [2, 25, 256], replicated, may hold values from -1.25 to 1.25
- coulomb: float32 [2, 256, 256], replicated, may hold values from -0.375 to 0.375
- rho_ij: float32 [512, 256], P(('dx', 'dyz')), may hold values from -6 to 6
- projections: float32 [512, 16, 512], P(('dx', 'dyz'), None, 'band'), may hold values from -6 to 6
Outputs:
- potential: float32 [64, 96, 512], P('dx', 'dyz', 'band')
- atom_hamiltonian: float32 [512, 256], P(('dx', 'dyz'))
- applied: float32 [512, 16, 512], P(('dx', 'dyz'), None, 'band')
Inputs may be any that keep to these rules, and one draw needn't show every extreme that they name: Atom a's first two box_root entries lie within the first- and second-dimension cells held by the devices that hold atom a; the third is any cell of the third dimension. Domain column c holds its atoms in slots c * 64 to c * 64 + atom_count[c] - 1; its other slots are empty.
All inputs are finite; a program needn't handle non-finite values. No bound on the sum of `atom_count` on one device may be relied on, other than what follows from the above.
Results may differ from a plain program's by a relative error of at most 0.0003.
Values sent between devices are 32-bit elements; how exact they have to be, the bound alone decides.
A program may use at most 64 MiB of HBM per device.

v0:
```python
import jax
import jax.numpy as jnp
from jax import lax
from jax.sharding import PartitionSpec as P

BOX = 16
NI = 16


GRID_H = 0.15
KAPPA = 0.804
MU_COEF = 0.2195149727645171
PRECISE = lax.Precision.HIGHEST


def padded_2(array, sides, width):
    for axis, dim in sides:
        devices, length = (lax.axis_size(axis), array.shape[dim])
        up = [(i, (i + 1) % devices) for i in range(devices)]
        down = [(j, i) for i, j in up]
        last = lax.slice_in_dim(array, length - width, length, axis=dim)
        leading = lax.slice_in_dim(array, 0, width, axis=dim)
        before = lax.ppermute(last, axis, up)
        after = lax.ppermute(leading, axis, down)
        array = jnp.concatenate([before, array, after], axis=dim)
    return array


def passed_along(block, axis, distance):
    devices = range(lax.axis_size(axis))
    route = [((i - distance) % len(devices), i) for i in devices]
    return lax.ppermute(block, axis, route)


def exchange_energy(dens, sigma):
    prefactor = -0.75 * (3.0 / jnp.pi) ** (1.0 / 3.0)
    reduced = sigma / (4.0 * (3.0 * jnp.pi**2) ** (2.0 / 3.0) * dens ** (8.0 / 3.0))
    enhance = 1.0 + KAPPA - KAPPA / (1.0 + MU_COEF * reduced / KAPPA)
    return prefactor * dens ** (4.0 / 3.0) * enhance


def energy_slopes(dens, sigma):

    def summed(dens_in, sigma_in):
        return jnp.sum(exchange_energy(dens_in, sigma_in))

    return jax.grad(summed, argnums=(0, 1))(dens, sigma)


def gradients(padded):
    half_step = 0.5 / GRID_H
    inner = padded[1:-1, 1:-1, 1:-1]
    grad_x = (padded[2:, 1:-1, 1:-1] - padded[:-2, 1:-1, 1:-1]) * half_step
    grad_y = (padded[1:-1, 2:, 1:-1] - padded[1:-1, :-2, 1:-1]) * half_step
    grad_z = (padded[1:-1, 1:-1, 2:] - padded[1:-1, 1:-1, :-2]) * half_step
    return (inner, grad_x, grad_y, grad_z)


def divergence(flux_x, flux_y, flux_z):
    half_step = 0.5 / GRID_H
    part_x = (flux_x[2:, 1:-1, 1:-1] - flux_x[:-2, 1:-1, 1:-1]) * half_step
    part_y = (flux_y[1:-1, 2:, 1:-1] - flux_y[1:-1, :-2, 1:-1]) * half_step
    part_z = (flux_z[1:-1, 1:-1, 2:] - flux_z[1:-1, 1:-1, :-2]) * half_step
    return part_x + part_y + part_z


def hamiltonian_blocks(moments, rho_rows, picks, live, coupling, coulomb):
    summed = jnp.zeros((moments.shape[0], coulomb.shape[2]), jnp.float32)
    for spec_id in range(coupling.shape[0]):
        term = jnp.dot(moments, coupling[spec_id], precision=PRECISE) + 2.0 * jnp.dot(
            rho_rows, coulomb[spec_id], precision=PRECISE
        )
        summed = summed + picks[:, spec_id : spec_id + 1] * term
    return jnp.where(live[:, None], summed, 0.0)


def fold_moments(source, plan, shape_functions, z_cells, depth_all):
    width_x, width_y, depth = source.shape
    box_steps = jnp.arange(BOX, dtype=jnp.int32)
    spec_count = shape_functions.shape[0]
    comp_count = shape_functions.shape[1]
    shaped = shape_functions.reshape(spec_count * comp_count, BOX, BOX, BOX)
    flat_source = source.reshape(width_x * width_y, depth)
    cells_x = jnp.arange(width_x, dtype=jnp.int32)
    cells_y = jnp.arange(width_y, dtype=jnp.int32)
    slots = plan.shape[1]
    group = 16
    turns = slots // group

    def block_moments(block_plan):
        offset = (z_cells[None, :] - block_plan[2][:, None]) % depth_all
        select_z = (offset[:, None, :] == box_steps[None, :, None]).astype(jnp.float32)
        select_z = select_z.reshape(group * BOX, depth)
        along_z = lax.dot_general(
            flat_source, select_z, (((1,), (1,)), ((), ())), precision=PRECISE
        )
        along_z = along_z.reshape(width_x, width_y, group, BOX)
        select_y = (
            cells_y[None, None, :] - block_plan[1][:, None, None] == box_steps[None, :, None]
        ).astype(jnp.float32)
        along_y = jnp.einsum("xyak,ajy->xjak", along_z, select_y, precision=PRECISE)
        select_x = (
            cells_x[None, None, :] - block_plan[0][:, None, None] == box_steps[None, :, None]
        ).astype(jnp.float32)
        select_x = select_x * block_plan[3][:, None, None].astype(jnp.float32)
        along_x = jnp.einsum("xjak,aix->ijak", along_y, select_x, precision=PRECISE)
        return jnp.einsum("sijk,ijak->as", shaped, along_x, precision=PRECISE)

    blocks_in = plan.reshape(5, turns, group).transpose(1, 0, 2)
    every = lax.map(block_moments, blocks_in)
    every = every.reshape(slots, spec_count, comp_count)
    picks = (plan[4][:, None] == jnp.arange(spec_count, dtype=jnp.int32)[None, :]).astype(
        jnp.float32
    )
    return jnp.sum(every * picks[:, :, None], axis=1) * GRID_H**3


def local(
    density,
    hartree,
    box_root,
    species,
    atom_count,
    shape_functions,
    coupling,
    coulomb,
    rho_ij,
    projections,
):
    padded = padded_2(density, (("dx", 0), ("dyz", 1), ("band", 2)), 1)
    inner, grad_x, grad_y, grad_z = gradients(padded)
    sigma = grad_x * grad_x + grad_y * grad_y + grad_z * grad_z
    slope_n, slope_s = energy_slopes(inner, sigma)
    fluxes = jnp.stack([slope_s * grad_x, slope_s * grad_y, slope_s * grad_z])
    flux_pad = padded_2(fluxes, (("dx", 1), ("dyz", 2), ("band", 3)), 1)
    spread = divergence(flux_pad[0], flux_pad[1], flux_pad[2])
    potential = hartree + slope_n - 2.0 * spread
    width_x, width_y, depth = potential.shape
    first_x = lax.axis_index("dx") * width_x
    first_y = lax.axis_index("dyz") * width_y
    depth_all = depth * lax.axis_size("band")
    z_cells = lax.axis_index("band") * depth + jnp.arange(depth, dtype=jnp.int32)
    atom_slots = box_root.shape[1]
    rim_first = passed_along(potential[:BOX], "dx", -1)
    widened = jnp.concatenate([potential, rim_first], 0)
    rim_second = passed_along(widened[:, :BOX], "dyz", -1)
    widened = jnp.concatenate([widened, rim_second], 1)
    ones = jnp.ones((atom_slots,), jnp.int32)
    plan = jnp.stack([box_root[0] - first_x, box_root[1] - first_y, box_root[2], ones, species])
    partial_value = fold_moments(widened, plan, shape_functions, z_cells, depth_all)
    spec_count = shape_functions.shape[0]
    picks = (species[:, None] == jnp.arange(spec_count, dtype=jnp.int32)[None, :]).astype(
        jnp.float32
    )
    live = jnp.arange(atom_slots, dtype=jnp.int32) < atom_count[0]
    moments = lax.psum(partial_value, "band")
    atom_hamiltonian = hamiltonian_blocks(moments, rho_ij, picks, live, coupling, coulomb)
    blocks = atom_hamiltonian.reshape(atom_slots, NI, NI)
    applied = jnp.einsum("aij,ajn->ain", blocks, projections, precision=PRECISE)
    return (potential, atom_hamiltonian, applied)


def solution(mesh):
    in_specs = (
        P("dx", "dyz", "band"),
        P("dx", "dyz", "band"),
        P(None, ("dx", "dyz")),
        P(("dx", "dyz")),
        P(("dx", "dyz")),
        P(),
        P(),
        P(),
        P(("dx", "dyz"), None),
        P(("dx", "dyz"), None, "band"),
    )
    out_specs = (P("dx", "dyz", "band"), P(("dx", "dyz"), None), P(("dx", "dyz"), None, "band"))
    return jax.shard_map(local, mesh=mesh, in_specs=in_specs, out_specs=out_specs, check_vma=False)
```

profile of v0, /device:TPU:0, one launch (start us, length us, event | category | flops | bytes accessed | tf_op | source)
XLA Modules:
  0.0 253.0 jit_solution(3494009617983660709)
XLA Ops:
  8.4 4.1 %collective-permute-start.2 = (f32[34,1,128]{2,1,0:T(1,128)S(1)}, f32[34,1,128]{2,1,0:T(1,128)S(1)}, u32[]{:S(2)}, u32[]{:S(2)}) collective-permute-start(f32[34,1,128]{2,1,0:T(1,128)S(1)} %get-tuple-element.225), channel_id=1, source_target_pairs={{1,0},{2,1},{3,2},{0,3},{5,4},{6,5},{7,6},{4,7},{9,8},{10,9},{11,1... | collective-permute-start | bytes 52232 | tf_op jit(solution)/shard_map/ppermute | solution.py:24
  13.9 4.1 %collective-permute-done.3 = f32[34,1,128]{2,1,0:T(1,128)S(1)} collective-permute-done((f32[34,1,128]{2,1,0:T(1,128)S(1)}, f32[34,1,128]{2,1,0:T(1,128)S(1)}, u32[]{:S(2)}, u32[]{:S(2)}) %collective-permute-start.3) | collective-permute-done | bytes 17440 | tf_op jit(solution)/shard_map/ppermute | solution.py:23
  52.6 5.4 %pad_maximum_fusion = f32[3,34,26,130]{3,2,1,0:T(8,128)S(1)} fusion(f32[3,34,26,1]{3,2,1,0:T(8,128)} %copy.54, f32[3,34,1,128]{3,2,1,0:T(1,128)S(1)} %collective-permute-done.9, f32[3,1,24,128]{3,2,1,0:T(8,128)S(1)} %collective-permute-done.7, f32[1,32,24,128]{3,2,1,0:T(8,128)S(1)} %get-tuple-element.228, f32[1,32,24,128]{3,2,1,0:T(8,128)S(1)} %get-tuple-element.227, ...), kind=kLoop, calls=%fused_computation.43 | loop fusion | flops 2758080 | bytes 2758080 | tf_op jit(solution)/shard_map/concatenate | solution.py:25
  61.4 6.3 %collective-permute-done.12 = f32[16,24,128]{2,1,0:T(8,128)S(1)} collective-permute-done((f32[16,24,128]{2,1,0:T(8,128)S(1)}, f32[16,24,128]{2,1,0:T(8,128)S(1)}, u32[]{:S(2)}, u32[]{:S(2)}) %collective-permute-start.12) | collective-permute-done | bytes 196640 | tf_op jit(solution)/shard_map/ppermute | solution.py:32
  71.8 5.8 %copy.55 = f32[2,25,4096]{1,0,2:T(2,128)} copy(f32[2,25,4096]{2,0,1:T(2,128)} %param.17) | data formatting | bytes 1638400 | tf_op args[5]
  77.6 5.5 %reshape.189 = f32[50,16,16,16]{0,3,2,1:T(8,128)} reshape(f32[2,25,4096]{1,0,2:T(2,128)} %copy.55) | data formatting | bytes 1638400 | tf_op jit(solution)/shard_map/reshape | solution.py:82
  84.5 155.5 %while.14 = (s32[]{:T(128)}, f32[4,16,50]{2,1,0:T(8,128)S(1)}, s32[4,5,16]{2,0,1:T(4,128)S(1)}, f32[1920,128]{1,0:T(8,128)}, f32[50,16,16,16]{0,3,2,1:T(8,128)},...) while((s32[]{:T(128)}, f32[4,16,50]{2,1,0:T(8,128)S(1)}, ...), condition=%wide.region_1.2_spmd.clone.clone, body=%wide.region_0.1_spmd.clone.clone.sunk | while | flops 926510592 | bytes 18260932 | solution.py:110
  87.0 6.0 %reshape.215 = f32[48,40,16,16]{1,0,3,2:T(8,128)} reshape(f32[1920,256]{0,1:T(8,128)S(1)} %convolution_bitcast_fusion.4) | data formatting | bytes 3932160 | tf_op jit(solution)/shard_map/while/body/eval_jaxpr/reshape | solution.py:97
  93.1 11.1 %convolution_bitcast_fusion.5 = f32[48,16,16,16]{0,1,3,2:T(8,128)S(1)} fusion(f32[48,40,16,16]{1,0,3,2:T(8,128)} %reshape.215, s32[16,40]{1,0:T(8,128)S(1)} %iota_subtract_fusion.4), kind=kOutput, calls=%fused_computation.10.clone.1 | convolution fusion | flops 94382080 | bytes 2755072 | tf_op jit(solution)/shard_map/while/body/eval_jaxpr/xyak,ajy->xjak/dot_general | solution.py:101
  104.2 14.7 %fusion.94 = f32[16,16,16,16]{3,0,1,2:T(8,128)S(1)} fusion(f32[48,16,16,16]{0,1,3,2:T(8,128)S(1)} %convolution_bitcast_fusion.5, f32[16]{0:T(128)S(1)} %get-tuple-element.278, s32[16,48]{1,0:T(8,128)S(1)} %iota_subtract_fusion.5), kind=kOutput, calls=%fused_computation.9.clone.1 | convolution fusion | flops 37773312 | bytes 1051712 | tf_op jit(solution)/shard_map/while/body/eval_jaxpr/xjak,aix->ijak/dot_general | solution.py:106
  119.0 4.4 %fusion.95 = f32[4,16,50]{2,1,0:T(8,128)S(1)} fusion(f32[4,16,50]{2,1,0:T(8,128)S(1)} %get-tuple-element.292, s32[]{:T(128)} %get-tuple-element.291, f32[50,16,16,16]{0,3,2,1:T(8,128)S(1)} %copy-done.1, f32[16,16,16,16]{3,0,1,2:T(8,128)S(1)} %fusion.94), kind=kOutput, calls=%fused_computation.12.clone.1 | convolution fusion | flops 39321600 | bytes 4202500 | tf_op jit(solution)/shard_map/while/body/eval_jaxpr/sijk,ijak->as/dot_general | solution.py:107
  125.9 6.0 %reshape.215 = f32[48,40,16,16]{1,0,3,2:T(8,128)} reshape(f32[1920,256]{0,1:T(8,128)S(1)} %convolution_bitcast_fusion.4) | data formatting | bytes 3932160 | tf_op jit(solution)/shard_map/while/body/eval_jaxpr/reshape | solution.py:97
  132.0 11.1 %convolution_bitcast_fusion.5 = f32[48,16,16,16]{0,1,3,2:T(8,128)S(1)} fusion(f32[48,40,16,16]{1,0,3,2:T(8,128)} %reshape.215, s32[16,40]{1,0:T(8,128)S(1)} %iota_subtract_fusion.4), kind=kOutput, calls=%fused_computation.10.clone.1 | convolution fusion | flops 94382080 | bytes 2755072 | tf_op jit(solution)/shard_map/while/body/eval_jaxpr/xyak,ajy->xjak/dot_general | solution.py:101
  143.1 14.7 %fusion.94 = f32[16,16,16,16]{3,0,1,2:T(8,128)S(1)} fusion(f32[48,16,16,16]{0,1,3,2:T(8,128)S(1)} %convolution_bitcast_fusion.5, f32[16]{0:T(128)S(1)} %get-tuple-element.278, s32[16,48]{1,0:T(8,128)S(1)} %iota_subtract_fusion.5), kind=kOutput, calls=%fused_computation.9.clone.1 | convolution fusion | flops 37773312 | bytes 1051712 | tf_op jit(solution)/shard_map/while/body/eval_jaxpr/xjak,aix->ijak/dot_general | solution.py:106
  157.9 4.4 %fusion.95 = f32[4,16,50]{2,1,0:T(8,128)S(1)} fusion(f32[4,16,50]{2,1,0:T(8,128)S(1)} %get-tuple-element.292, s32[]{:T(128)} %get-tuple-element.291, f32[50,16,16,16]{0,3,2,1:T(8,128)S(1)} %copy-done.1, f32[16,16,16,16]{3,0,1,2:T(8,128)S(1)} %fusion.94), kind=kOutput, calls=%fused_computation.12.clone.1 | convolution fusion | flops 39321600 | bytes 4202500 | tf_op jit(solution)/shard_map/while/body/eval_jaxpr/sijk,ijak->as/dot_general | solution.py:107
  164.8 6.0 %reshape.215 = f32[48,40,16,16]{1,0,3,2:T(8,128)} reshape(f32[1920,256]{0,1:T(8,128)S(1)} %convolution_bitcast_fusion.4) | data formatting | bytes 3932160 | tf_op jit(solution)/shard_map/while/body/eval_jaxpr/reshape | solution.py:97
  170.9 11.1 %convolution_bitcast_fusion.5 = f32[48,16,16,16]{0,1,3,2:T(8,128)S(1)} fusion(f32[48,40,16,16]{1,0,3,2:T(8,128)} %reshape.215, s32[16,40]{1,0:T(8,128)S(1)} %iota_subtract_fusion.4), kind=kOutput, calls=%fused_computation.10.clone.1 | convolution fusion | flops 94382080 | bytes 2755072 | tf_op jit(solution)/shard_map/while/body/eval_jaxpr/xyak,ajy->xjak/dot_general | solution.py:101
  182.0 14.7 %fusion.94 = f32[16,16,16,16]{3,0,1,2:T(8,128)S(1)} fusion(f32[48,16,16,16]{0,1,3,2:T(8,128)S(1)} %convolution_bitcast_fusion.5, f32[16]{0:T(128)S(1)} %get-tuple-element.278, s32[16,48]{1,0:T(8,128)S(1)} %iota_subtract_fusion.5), kind=kOutput, calls=%fused_computation.9.clone.1 | convolution fusion | flops 37773312 | bytes 1051712 | tf_op jit(solution)/shard_map/while/body/eval_jaxpr/xjak,aix->ijak/dot_general | solution.py:106
  196.7 4.4 %fusion.95 = f32[4,16,50]{2,1,0:T(8,128)S(1)} fusion(f32[4,16,50]{2,1,0:T(8,128)S(1)} %get-tuple-element.292, s32[]{:T(128)} %get-tuple-element.291, f32[50,16,16,16]{0,3,2,1:T(8,128)S(1)} %copy-done.1, f32[16,16,16,16]{3,0,1,2:T(8,128)S(1)} %fusion.94), kind=kOutput, calls=%fused_computation.12.clone.1 | convolution fusion | flops 39321600 | bytes 4202500 | tf_op jit(solution)/shard_map/while/body/eval_jaxpr/sijk,ijak->as/dot_general | solution.py:107
  203.6 6.0 %reshape.215 = f32[48,40,16,16]{1,0,3,2:T(8,128)} reshape(f32[1920,256]{0,1:T(8,128)S(1)} %convolution_bitcast_fusion.4) | data formatting | bytes 3932160 | tf_op jit(solution)/shard_map/while/body/eval_jaxpr/reshape | solution.py:97
  209.8 11.1 %convolution_bitcast_fusion.5 = f32[48,16,16,16]{0,1,3,2:T(8,128)S(1)} fusion(f32[48,40,16,16]{1,0,3,2:T(8,128)} %reshape.215, s32[16,40]{1,0:T(8,128)S(1)} %iota_subtract_fusion.4), kind=kOutput, calls=%fused_computation.10.clone.1 | convolution fusion | flops 94382080 | bytes 2755072 | tf_op jit(solution)/shard_map/while/body/eval_jaxpr/xyak,ajy->xjak/dot_general | solution.py:101
  220.9 14.7 %fusion.94 = f32[16,16,16,16]{3,0,1,2:T(8,128)S(1)} fusion(f32[48,16,16,16]{0,1,3,2:T(8,128)S(1)} %convolution_bitcast_fusion.5, f32[16]{0:T(128)S(1)} %get-tuple-element.278, s32[16,48]{1,0:T(8,128)S(1)} %iota_subtract_fusion.5), kind=kOutput, calls=%fused_computation.9.clone.1 | convolution fusion | flops 37773312 | bytes 1051712 | tf_op jit(solution)/shard_map/while/body/eval_jaxpr/xjak,aix->ijak/dot_general | solution.py:106
  235.6 4.4 %fusion.95 = f32[4,16,50]{2,1,0:T(8,128)S(1)} fusion(f32[4,16,50]{2,1,0:T(8,128)S(1)} %get-tuple-element.292, s32[]{:T(128)} %get-tuple-element.291, f32[50,16,16,16]{0,3,2,1:T(8,128)S(1)} %copy-done.1, f32[16,16,16,16]{3,0,1,2:T(8,128)S(1)} %fusion.94), kind=kOutput, calls=%fused_computation.12.clone.1 | convolution fusion | flops 39321600 | bytes 4202500 | tf_op jit(solution)/shard_map/while/body/eval_jaxpr/sijk,ijak->as/dot_general | solution.py:107
  240.4 10.4 %psum.7 = f32[64,25]{1,0:T(8,128)S(1)} all-reduce(f32[64,25]{1,0:T(8,128)S(1)} %broadcast_multiply_fusion), channel_id=1, replica_groups=mesh['band'=4,'dx'=2,'dyz'=4] {'band'}, use_global_device_ids=true, to_apply=%region_3.4 | all-reduce | flops 1600 | bytes 12800 | tf_op jit(solution)/shard_map/psum | solution.py:156
  (141 shorter events, 64.5 us)
Async XLA Ops:
  0.6 250.9 %copy-start = (f32[64,16,128]{2,1,0:T(8,128)S(1)}, f32[64,16,128]{2,1,0:T(8,128)}, u32[]{:S(2)}) copy-start(f32[64,16,128]{2,1,0:T(8,128)} %param.21) | copy-start | bytes 1572868
  1.4 5.8 %collective-permute-start.1 = (f32[1,24,128]{2,1,0:T(8,128)S(1)}, f32[1,24,128]{2,1,0:T(8,128)S(1)}, u32[]{:S(2)}, u32[]{:S(2)}) collective-permute-start(f32[1,24,128]{2,1,0:T(8,128)S(1)} %get-tuple-element.230), channel_id=1, source_target_pairs={{0,4},{4,0},{1,5},{5,1},{2,6},{6,2},{3,7},{7,3},{8,12},{12,8},{9,1... | collective-permute-start | bytes 36872 | tf_op jit(solution)/shard_map/ppermute | solution.py:23
  4.4 3.9 %collective-permute-start = (f32[1,24,128]{2,1,0:T(8,128)S(1)}, f32[1,24,128]{2,1,0:T(8,128)S(1)}, u32[]{:S(2)}, u32[]{:S(2)}) collective-permute-start(f32[1,24,128]{2,1,0:T(8,128)S(1)} %get-tuple-element.229), channel_id=1, source_target_pairs={{4,0},{0,4},{5,1},{1,5},{6,2},{2,6},{7,3},{3,7},{12,8},{8,12},{13,... | collective-permute-start | bytes 36872 | tf_op jit(solution)/shard_map/ppermute | solution.py:24
  8.4 5.6 %collective-permute-start.2 = (f32[34,1,128]{2,1,0:T(1,128)S(1)}, f32[34,1,128]{2,1,0:T(1,128)S(1)}, u32[]{:S(2)}, u32[]{:S(2)}) collective-permute-start(f32[34,1,128]{2,1,0:T(1,128)S(1)} %get-tuple-element.225), channel_id=1, source_target_pairs={{1,0},{2,1},{3,2},{0,3},{5,4},{6,5},{7,6},{4,7},{9,8},{10,9},{11,1... | collective-permute-start | bytes 52232 | tf_op jit(solution)/shard_map/ppermute | solution.py:24
  12.5 5.5 %collective-permute-start.3 = (f32[34,1,128]{2,1,0:T(1,128)S(1)}, f32[34,1,128]{2,1,0:T(1,128)S(1)}, u32[]{:S(2)}, u32[]{:S(2)}) collective-permute-start(f32[34,1,128]{2,1,0:T(1,128)S(1)} %get-tuple-element.226), channel_id=1, source_target_pairs={{0,1},{1,2},{2,3},{3,0},{4,5},{5,6},{6,7},{7,4},{8,9},{9,10},{10,1... | collective-permute-start | bytes 52232 | tf_op jit(solution)/shard_map/ppermute | solution.py:23
  18.7 1.5 collective-permute-start.4
  19.1 3.2 %collective-permute-start.5 = (f32[34,26,1]{0,2,1:T(1,128)S(1)}, f32[34,26,1]{0,2,1:T(1,128)S(1)}, u32[]{:S(2)}, u32[]{:S(2)}) collective-permute-start(f32[34,26,1]{0,2,1:T(1,128)S(1)} %copy.49), channel_id=1, source_target_pairs={{0,8},{8,16},{16,24},{24,0},{1,9},{9,17},{17,25},{25,1},{2,10},{10... | collective-permute-start | bytes 10616 | tf_op jit(solution)/shard_map/ppermute | solution.py:23
  25.8 5.8 %copy-start.4 = (f32[32,24,128]{2,1,0:T(8,128)}, f32[32,24,128]{2,1,0:T(8,128)S(1)}, u32[]{:S(2)}) copy-start(f32[32,24,128]{2,1,0:T(8,128)S(1)} %get-tuple-element.209) | copy-start | bytes 1179652
  26.1 4.1 %collective-permute-start.6 = (f32[3,1,24,128]{3,2,1,0:T(8,128)S(1)}, f32[3,1,24,128]{3,2,1,0:T(8,128)S(1)}, u32[]{:S(2)}, u32[]{:S(2)}) collective-permute-start(f32[3,1,24,128]{3,2,1,0:T(8,128)S(1)} %get-tuple-element.221), channel_id=1, source_target_pairs={{0,4},{4,0},{1,5},{5,1},{2,6},{6,2},{3,7},{7,3},{8,12},{12,8},{9,1... | collective-permute-start | bytes 110600 | tf_op jit(solution)/shard_map/ppermute | solution.py:23
  27.6 4.0 %collective-permute-start.7 = (f32[3,1,24,128]{3,2,1,0:T(8,128)S(1)}, f32[3,1,24,128]{3,2,1,0:T(8,128)S(1)}, u32[]{:S(2)}, u32[]{:S(2)}) collective-permute-start(f32[3,1,24,128]{3,2,1,0:T(8,128)S(1)} %get-tuple-element.222), channel_id=1, source_target_pairs={{4,0},{0,4},{5,1},{1,5},{6,2},{2,6},{7,3},{3,7},{12,8},{8,12},{13,... | collective-permute-start | bytes 110600 | tf_op jit(solution)/shard_map/ppermute | solution.py:24
  31.7 6.0 %collective-permute-start.8 = (f32[3,34,1,128]{3,2,1,0:T(1,128)S(1)}, f32[3,34,1,128]{3,2,1,0:T(1,128)S(1)}, u32[]{:S(2)}, u32[]{:S(2)}) collective-permute-start(f32[3,34,1,128]{3,2,1,0:T(1,128)S(1)} %get-tuple-element.219), channel_id=1, source_target_pairs={{0,1},{1,2},{2,3},{3,0},{4,5},{5,6},{6,7},{7,4},{8,9},{9,10},{10,1... | collective-permute-start | bytes 156680 | tf_op jit(solution)/shard_map/ppermute | solution.py:23
  31.7 5.9 %collective-permute-start.9 = (f32[3,34,1,128]{3,2,1,0:T(1,128)S(1)}, f32[3,34,1,128]{3,2,1,0:T(1,128)S(1)}, u32[]{:S(2)}, u32[]{:S(2)}) collective-permute-start(f32[3,34,1,128]{3,2,1,0:T(1,128)S(1)} %get-tuple-element.220), channel_id=1, source_target_pairs={{1,0},{2,1},{3,2},{0,3},{5,4},{6,5},{7,6},{4,7},{9,8},{10,9},{11,1... | collective-permute-start | bytes 156680 | tf_op jit(solution)/shard_map/ppermute | solution.py:24
  42.5 4.9 %collective-permute-start.10 = (f32[3,34,26,1]{1,3,2,0:T(1,128)S(1)}, f32[3,34,26,1]{1,3,2,0:T(1,128)S(1)}, u32[]{:S(2)}, u32[]{:S(2)}) collective-permute-start(f32[3,34,26,1]{1,3,2,0:T(1,128)S(1)} %copy.51), channel_id=1, source_target_pairs={{0,8},{8,16},{16,24},{24,0},{1,9},{9,17},{17,25},{25,1},{2,10},{10... | collective-permute-start | bytes 31832 | tf_op jit(solution)/shard_map/ppermute | solution.py:23
  44.8 5.2 %collective-permute-start.11 = (f32[3,34,26,1]{1,3,2,0:T(1,128)S(1)}, f32[3,34,26,1]{1,3,2,0:T(1,128)S(1)}, u32[]{:S(2)}, u32[]{:S(2)}) collective-permute-start(f32[3,34,26,1]{1,3,2,0:T(1,128)S(1)} %copy.52), channel_id=1, source_target_pairs={{8,0},{16,8},{24,16},{0,24},{9,1},{17,9},{25,17},{1,25},{10,2},{18... | collective-permute-start | bytes 31832 | tf_op jit(solution)/shard_map/ppermute | solution.py:24
  59.1 12.4 %copy-start.10 = (s32[64]{0:T(128)S(1)}, s32[64]{0:T(128)}, u32[]{:S(2)}) copy-start(s32[64]{0:T(128)} %param.15) | copy-start | bytes 772
  60.7 22.6 %copy-start.2 = (f32[32,24,128]{2,1,0:T(8,128)}, f32[32,24,128]{2,1,0:T(8,128)S(1)}, u32[]{:S(2)}) copy-start(f32[32,24,128]{2,1,0:T(8,128)S(1)} %fusion.43) | copy-start | bytes 1179652
  60.8 6.9 %collective-permute-start.12 = (f32[16,24,128]{2,1,0:T(8,128)S(1)}, f32[16,24,128]{2,1,0:T(8,128)S(1)}, u32[]{:S(2)}, u32[]{:S(2)}) collective-permute-start(f32[16,24,128]{2,1,0:T(8,128)S(1)} %slice.209), channel_id=1, source_target_pairs={{4,0},{0,4},{5,1},{1,5},{6,2},{2,6},{7,3},{3,7},{12,8},{8,12},{13,... | collective-permute-start | bytes 589832 | tf_op jit(solution)/shard_map/ppermute | solution.py:32
  67.7 15.7 %collective-permute-start.13 = (f32[48,16,128]{2,1,0:T(8,128)S(1)}, f32[48,16,128]{2,1,0:T(8,128)S(1)}, u32[]{:S(2)}, u32[]{:S(2)}) collective-permute-start(f32[48,16,128]{2,1,0:T(8,128)S(1)} %pad_maximum_fusion.4), channel_id=1, source_target_pairs={{1,0},{2,1},{3,2},{0,3},{5,4},{6,5},{7,6},{4,7},{9,8},{10,9},{11,1... | collective-permute-start | bytes 1179656 | tf_op jit(solution)/shard_map/ppermute | solution.py:32
  77.6 5.5 %copy-start.6 = (f32[2,256,256]{2,1,0:T(8,128)S(1)}, f32[2,256,256]{2,1,0:T(8,128)}, u32[]{:S(2)}) copy-start(f32[2,256,256]{2,1,0:T(8,128)} %param.19) | copy-start | bytes 1572868
  77.6 5.5 %copy-start.9 = (f32[64,256]{1,0:T(8,128)S(1)}, f32[64,256]{1,0:T(8,128)}, u32[]{:S(2)}) copy-start(f32[64,256]{1,0:T(8,128)} %param.20) | copy-start | bytes 196612
  104.2 14.8 %copy-start.1 = (f32[50,16,16,16]{0,3,2,1:T(8,128)S(1)}, f32[50,16,16,16]{0,3,2,1:T(8,128)}, u32[]{:S(2)}) copy-start(f32[50,16,16,16]{0,3,2,1:T(8,128)} %get-tuple-element.306) | copy-start | bytes 2457604 | tf_op jit(solution)/shard_map/while
  143.1 14.8 %copy-start.1 = (f32[50,16,16,16]{0,3,2,1:T(8,128)S(1)}, f32[50,16,16,16]{0,3,2,1:T(8,128)}, u32[]{:S(2)}) copy-start(f32[50,16,16,16]{0,3,2,1:T(8,128)} %get-tuple-element.306) | copy-start | bytes 2457604 | tf_op jit(solution)/shard_map/while
  182.0 14.8 %copy-start.1 = (f32[50,16,16,16]{0,3,2,1:T(8,128)S(1)}, f32[50,16,16,16]{0,3,2,1:T(8,128)}, u32[]{:S(2)}) copy-start(f32[50,16,16,16]{0,3,2,1:T(8,128)} %get-tuple-element.306) | copy-start | bytes 2457604 | tf_op jit(solution)/shard_map/while
  220.9 14.8 %copy-start.1 = (f32[50,16,16,16]{0,3,2,1:T(8,128)S(1)}, f32[50,16,16,16]{0,3,2,1:T(8,128)}, u32[]{:S(2)}) copy-start(f32[50,16,16,16]{0,3,2,1:T(8,128)} %get-tuple-element.306) | copy-start | bytes 2457604 | tf_op jit(solution)/shard_map/while
  (4 other events, 9.5 us)
where the time goes:
time: 254 us; the launch traced here: 253 us
  matrix products  133 us (52%)
  local copies, waits for them, and re-layouts  55.6 us (22%)
  starting transfers between devices  20.1 us (8%)
  waiting for transfers between devices  18.4 us (7%)
  other arithmetic  14 us (6%)
  blocking collectives  10.4 us (4%)
    dot_general x4, matrix products, block_moments(): along_x = jnp.einsum('xjak,aix->ijak', along_y, select_x, precision=PRECISE)  59 us
    dot_general x4, matrix products, block_moments(): along_y = jnp.einsum('xyak,ajy->xjak', along_z, select_y, precision=PRECISE)  44.2 us
    reshape x4, local copies, waits for them, and re-layouts, block_moments(): along_z = along_z.reshape(width_x, width_y, group, BOX)  24.1 us
    dot_general x4, matrix products, block_moments(): return jnp.einsum('sijk,ijak->as', shaped, along_x, precision=PRECISE)  17.7 us
    ppermute x6, starting transfers between devices, padded_2(): after = lax.ppermute(leading, axis, down)  10.5 us
    psum x1, blocking collectives, local(): moments = lax.psum(partial_value, 'band')  10.4 us
    ppermute x6, waiting for transfers between devices, padded_2(): before = lax.ppermute(last, axis, up)  9.63 us
    dot_general x4, matrix products, block_moments(): lax.dot_general(flat_source, select_z, (((1,), (1,)), ((), ())), precisio...  8.6 us
  transfers between devices with their start and end apart: 14, of which 8 were waited for; matrix products, arithmetic and copies ran while one was open for 9% of the time, Pallas kernels for 0%

commit v1 on v0

v1 whole, which is shorter than its diff:
```python
import functools
import math

import jax
import jax.numpy as jnp
from jax import lax
from jax.experimental import pallas as pl
from jax.experimental.pallas import tpu as pltpu
from jax.sharding import PartitionSpec as P

BOX = 16
NI = 16
GROUP = 16
PAD = 16
GRID_H = 0.15
KAPPA = 0.804
MU_COEF = 0.2195149727645171
PRECISE = lax.Precision.HIGHEST
HALF = 0.5 / GRID_H
PREF = -0.75 * (3.0 / math.pi) ** (1.0 / 3.0)
RED = 4.0 * (3.0 * math.pi**2) ** (2.0 / 3.0)
MESH = pl.DeviceIdType.MESH
VMEM_LIMIT = 48 * 1024 * 1024


def iota(shape, dim):
    return lax.broadcasted_iota(jnp.int32, shape, dim)


def shifted(axis, step):
    size = lax.axis_size(axis)
    return lax.rem(lax.axis_index(axis) + (step + size), size)


def enter(devices):
    barrier = pltpu.get_barrier_semaphore()
    for device in devices:
        pl.semaphore_signal(barrier, inc=1, device_id=device, device_id_type=MESH)
    pl.semaphore_wait(barrier, len(devices))


def split(value):
    high = value.astype(jnp.bfloat16)
    return high, (value - high.astype(jnp.float32)).astype(jnp.bfloat16)


def mm(a, b):
    return jnp.dot(a, b, preferred_element_type=jnp.float32)


def pack_ends(ref):
    wx, wy, depth = ref.shape
    lane = iota((wy, depth), 1)
    packed = jnp.zeros((wy, depth), jnp.float32)
    for x in range(wx):
        moved = pltpu.roll(ref[x], 2 * x + 1, 1)
        packed = jnp.where((lane == 2 * x) | (lane == 2 * x + 1), moved, packed)
    return packed


def join_ends(before, after):
    lane = iota(before.shape, 1)
    depth = before.shape[1]
    return jnp.where(
        lax.rem(lane, 2) == 1, pltpu.roll(before, 1, 1), pltpu.roll(after, depth - 1, 1)
    )


def grid_kernel(
    dens_ref, hart_ref, root_ref, species_ref, count_ref,
    pot_ref, list_ref,
    dpad, fxp, fyp, fz, slope_n_ref,
    send_x, send_y, send_z, recv_x, recv_y, recv_z,
    gsend_x, gsend_y, gsend_z, grecv_x, grecv_y, grecv_z,
    plan_send, plan_recv, send_sems, recv_sems,
):
    wx, wy, depth = dens_ref.shape
    up_x, down_x = {"dx": shifted("dx", 1)}, {"dx": shifted("dx", -1)}
    up_y, down_y = {"dyz": shifted("dyz", 1)}, {"dyz": shifted("dyz", -1)}
    up_z, down_z = {"band": shifted("band", 1)}, {"band": shifted("band", -1)}
    up_xy = {"dx": shifted("dx", 1), "dyz": shifted("dyz", 1)}
    down_xy = {"dx": shifted("dx", -1), "dyz": shifted("dyz", -1)}
    slots = root_ref.shape[1]

    def remote(src, dst, sem, device):
        copy = pltpu.make_async_remote_copy(
            src_ref=src, dst_ref=dst, send_sem=send_sems.at[sem], recv_sem=recv_sems.at[sem],
            device_id=device, device_id_type=MESH,
        )
        copy.start()
        return copy

    send_x[0] = dens_ref[wx - 1]
    send_x[1] = dens_ref[0]
    send_y[0] = dens_ref[:, wy - 1, :]
    send_y[1] = dens_ref[:, 0, :]
    send_z[...] = pack_ends(dens_ref)
    plan_send[...] = jnp.zeros_like(plan_send)
    plan_send[0:1, 0:slots] = root_ref[0:1, :] - lax.axis_index("dx") * wx
    plan_send[1:2, 0:slots] = root_ref[1:2, :] - lax.axis_index("dyz") * wy
    plan_send[2:3, 0:slots] = root_ref[2:3, :]
    plan_send[3:4, 0:slots] = species_ref[...]
    plan_send[4:5, :] = jnp.full((1, 128), count_ref[0], jnp.int32)

    enter([up_x, down_x, up_y, down_y, up_z, down_z, up_xy, down_xy])
    first = [
        remote(send_z, recv_z.at[0], 0, up_z),
        remote(send_z, recv_z.at[1], 1, down_z),
        remote(send_y.at[0], recv_y.at[0], 2, up_y),
        remote(send_y.at[1], recv_y.at[1], 3, down_y),
        remote(send_x.at[0], recv_x.at[0], 4, up_x),
        remote(send_x.at[1], recv_x.at[1], 5, down_x),
    ]
    plans = [
        remote(plan_send, plan_recv.at[0], 6, up_x),
        remote(plan_send, plan_recv.at[1], 7, up_y),
        remote(plan_send, plan_recv.at[2], 8, up_xy),
    ]
    dpad[1 : wx + 1, 8 : wy + 8, :] = dens_ref[...]
    for copy in first:
        copy.wait()
    dpad[0, 8 : wy + 8, :] = recv_x[0]
    dpad[wx + 1, 8 : wy + 8, :] = recv_x[1]
    dpad[1 : wx + 1, 7, :] = recv_y[0]
    dpad[1 : wx + 1, wy + 8, :] = recv_y[1]
    ends = join_ends(recv_z[0], recv_z[1])
    lane = iota((wy, depth), 1)

    def flux_step(x):
        here = dpad[x + 1, 8 : wy + 8, :]
        gx = (dpad[x + 2, 8 : wy + 8, :] - dpad[x, 8 : wy + 8, :]) * HALF
        gy = (dpad[x + 1, 9 : wy + 9, :] - dpad[x + 1, 7 : wy + 7, :]) * HALF
        end = pltpu.roll(ends, depth - 1 - 2 * x, 1)
        after = jnp.where(lane == depth - 1, end, pltpu.roll(here, depth - 1, 1))
        before = jnp.where(lane == 0, end, pltpu.roll(here, 1, 1))
        gz = (after - before) * HALF
        sigma = gx * gx + gy * gy + gz * gz
        log_n = jnp.log(here)
        cube = jnp.exp(log_n * (1.0 / 3.0))
        inv = 1.0 / (here * cube)
        r = sigma * inv * inv * (1.0 / RED)
        u = 1.0 / (1.0 + (MU_COEF / KAPPA) * r)
        slope_r = MU_COEF * u * u
        slope_s = (PREF / RED) * slope_r * inv
        enhance = 1.0 + KAPPA - KAPPA * u
        slope_n_ref[x] = (4.0 / 3.0 * PREF) * cube * (enhance - 2.0 * r * slope_r)
        fxp[x + 1] = slope_s * gx
        fyp[x, 8 : wy + 8, :] = slope_s * gy
        fz[x] = slope_s * gz

    per = 4

    def flux_steps(t, carry):
        for k in range(per):
            flux_step(t * per + k)
        return carry

    lax.fori_loop(0, wx // per, flux_steps, 0)

    gsend_x[0] = fxp[wx]
    gsend_x[1] = fxp[1]
    gsend_y[0] = fyp[:, wy + 7, :]
    gsend_y[1] = fyp[:, 8, :]
    gsend_z[...] = pack_ends(fz)
    second = [
        remote(gsend_z, grecv_z.at[0], 9, up_z),
        remote(gsend_z, grecv_z.at[1], 10, down_z),
        remote(gsend_y.at[0], grecv_y.at[0], 11, up_y),
        remote(gsend_y.at[1], grecv_y.at[1], 12, down_y),
        remote(gsend_x.at[0], grecv_x.at[0], 13, up_x),
        remote(gsend_x.at[1], grecv_x.at[1], 14, down_x),
    ]

    for copy in plans:
        copy.wait()
    depth_all = depth * lax.axis_size("band")
    first_z = lax.axis_index("band") * depth
    columns = []
    for c in range(4):
        plan = plan_send[...] if c == 0 else plan_recv[c - 1]
        x = plan[0:1, :] - (wx if c in (1, 3) else 0)
        y = plan[1:2, :] - (wy if c in (2, 3) else 0)
        z = plan[2:3, :] - first_z
        z = jnp.where(z < 0, z + depth_all, z)
        slot = iota((1, 128), 1)
        meets = (slot < plan[4:5, :]) & (slot < slots)
        meets &= (x > -BOX) & (y > -BOX) & (x < wx) & (y < wy)
        meets &= (z < depth) | (z > depth_all - BOX)
        rows = (x + PAD) * (wy + 2 * PAD) + (y + PAD)
        dest = 8 + c * slots + slot
        columns.append((meets, rows, z, dest, plan[3:4, :]))
    meets, rows, z, dest, kind = [jnp.concatenate([c[f].astype(jnp.int32) for c in columns], 1) for f in range(5)]
    wide = 4 * 128
    upper = (iota((wide, wide), 0) <= iota((wide, wide), 1)).astype(jnp.bfloat16)
    row8 = iota((8, wide), 0)
    picked = jnp.where((meets == 1) & (kind == row8), 1.0, 0.0)
    order = mm(picked.astype(jnp.bfloat16), upper)
    fields = jnp.where(row8 == 0, rows, jnp.where(row8 == 1, z, jnp.where(row8 == 2, dest, 0)))
    fields = fields.astype(jnp.float32)
    for s in range(2):
        total = jnp.sum(picked[s : s + 1, :], axis=1, keepdims=True)
        place = iota((256, wide), 0).astype(jnp.float32) + 1.0
        onehot = jnp.where((order[s : s + 1, :] == place) & (picked[s : s + 1, :] > 0.5), 1.0, 0.0)
        got = lax.dot_general(
            fields, onehot, (((1,), (1,)), ((), ())), precision=PRECISE,
            preferred_element_type=jnp.float32,
        )
        got = jnp.where(iota((8, 256), 0) == 3, total, got)
        list_ref[s] = (got + 0.5).astype(jnp.int32)

    for copy in second:
        copy.wait()
    fxp[0] = grecv_x[0]
    fxp[wx + 1] = grecv_x[1]
    fyp[:, 7, :] = grecv_y[0]
    fyp[:, wy + 8, :] = grecv_y[1]
    flux_ends = join_ends(grecv_z[0], grecv_z[1])

    def pot_step(x):
        here = fz[x]
        end = pltpu.roll(flux_ends, depth - 1 - 2 * x, 1)
        after = jnp.where(lane == depth - 1, end, pltpu.roll(here, depth - 1, 1))
        before = jnp.where(lane == 0, end, pltpu.roll(here, 1, 1))
        spread = (fxp[x + 2] - fxp[x]) * HALF
        spread = spread + (fyp[x, 9 : wy + 9, :] - fyp[x, 7 : wy + 7, :]) * HALF
        spread = spread + (after - before) * HALF
        pot_ref[x] = hart_ref[x] + slope_n_ref[x] - 2.0 * spread

    def pot_steps(t, carry):
        for k in range(per):
            pot_step(t * per + k)
        return carry

    lax.fori_loop(0, wx // per, pot_steps, 0)


def moment_kernel(
    depth_all, list_ref, pot_ref, high_ref, low_ref, out_pot_ref, out_ref, padded, gathered, folded, sums
):
    wx, wy, depth = pot_ref.shape
    rows_y = wy + 2 * PAD
    comps = high_ref.shape[1] // BOX
    out_pot_ref[...] = pot_ref[...]
    padded[...] = jnp.zeros_like(padded)
    for x in range(wx):
        start = (x + PAD) * rows_y + PAD
        padded[start : start + wy, :] = pot_ref[x]
    sums[...] = jnp.zeros_like(sums)
    folded[...] = jnp.zeros_like(folded)
    lanes = GROUP * BOX
    lane = iota((BOX, 128), 1)
    adder = (iota((GROUP, lanes), 0) == iota((GROUP, lanes), 1) // BOX).astype(jnp.float32)
    keep = lax.rem(iota((BOX, lanes), 1), BOX) == iota((BOX, lanes), 0)

    for s in range(2):
        total = list_ref[s, 3, 0]

        def one_group(g, carry, s=s, total=total):
            gathered[...] = jnp.zeros_like(gathered)
            for q in range(GROUP):
                p = g * GROUP + q

                @pl.when(p < total)
                def _(q=q, p=p):
                    row = list_ref[s, 0, p]
                    z = list_ref[s, 1, p]
                    left = (q * BOX) % 128
                    tile = q * BOX // 128 * 128
                    shift = lax.rem(left + depth_all - z, depth)
                    cell = z + lane - left
                    cell = jnp.where(cell >= depth_all, cell - depth_all, cell)
                    mine = (lane >= left) & (lane < left + BOX) & (cell < depth)
                    for i in range(BOX):
                        piece = padded[pl.ds(row + i * rows_y, BOX), :]
                        piece = pltpu.roll(piece, shift, 1)
                        spot = (slice(i * BOX, (i + 1) * BOX), slice(tile, tile + 128))
                        gathered[spot] = jnp.where(mine, piece, gathered[spot])

            g_high, g_low = split(gathered[...])
            product = mm(high_ref[s], g_high) + (mm(high_ref[s], g_low) + mm(low_ref[s], g_high))
            product = jnp.where(keep[None], product.reshape(comps, BOX, lanes), 0.0)
            folded[0:comps, :] = jnp.sum(product, axis=1)
            result = lax.dot_general(
                adder, folded[...], (((1,), (1,)), ((), ())), precision=PRECISE,
                preferred_element_type=jnp.float32,
            ) * (GRID_H**3)
            for q in range(GROUP):
                spot = list_ref[s, 2, g * GROUP + q]
                sums[pl.ds(spot, 1), :] = result[q : q + 1, :]
            return carry

        lax.fori_loop(0, (total + GROUP - 1) // GROUP, one_group, 0)
    slots = out_ref.shape[1]
    for c in range(4):
        out_ref[c] = sums[8 + c * slots : 8 + (c + 1) * slots, :]


def block_kernel(
    part_ref, species_ref, count_ref, coupling_ref, coulomb_ref, rho_ref, ham_ref,
    around, parts, total_ref, cpad, send_sems, recv_sems,
):
    bands = lax.axis_size("band")
    me = lax.axis_index("band")
    slots = part_ref.shape[1]
    up_x, down_x = {"dx": shifted("dx", 1)}, {"dx": shifted("dx", -1)}
    up_y, down_y = {"dyz": shifted("dyz", 1)}, {"dyz": shifted("dyz", -1)}
    up_xy = {"dx": shifted("dx", 1), "dyz": shifted("dyz", 1)}
    down_xy = {"dx": shifted("dx", -1), "dyz": shifted("dyz", -1)}
    others = [{"band": shifted("band", t)} for t in range(1, bands)]
    enter([up_x, down_x, up_y, down_y, up_xy, down_xy] + others)

    def remote(src, dst, sem, device):
        copy = pltpu.make_async_remote_copy(
            src_ref=src, dst_ref=dst, send_sem=send_sems.at[sem], recv_sem=recv_sems.at[sem],
            device_id=device, device_id_type=MESH,
        )
        copy.start()
        return copy

    copies = [
        remote(part_ref.at[c + 1], around.at[c], c, device)
        for c, device in enumerate((down_x, down_y, down_xy))
    ]
    eye = iota((slots, slots), 0) == iota((slots, slots), 1)
    kind = jnp.sum(jnp.where(eye, species_ref[...], 0), axis=1, keepdims=True)
    live = iota((slots, 1), 0) < count_ref[0]
    cpad[...] = jnp.zeros_like(cpad)
    comps = coupling_ref.shape[1]
    rho_high, rho_low = split(rho_ref[...])
    coul = jnp.zeros(rho_ref.shape, jnp.float32)
    for s in range(2):
        cpad[s, 0:comps, :] = coupling_ref[s]
        c_high, c_low = split(coulomb_ref[s])
        term = mm(rho_high, c_high) + (mm(rho_high, c_low) + mm(rho_low, c_high))
        coul = jnp.where(kind == s, 2.0 * term, coul)
    for copy in copies:
        copy.wait()
    mine = (part_ref[0] + around[0]) + (around[1] + around[2])
    total_ref[...] = mine
    parts[me] = mine
    copies = [
        remote(total_ref, parts.at[me], 2 + t, others[t - 1]) for t in range(1, bands)
    ]
    for copy in copies:
        copy.wait()
    moments = (parts[0] + parts[1]) + (parts[2] + parts[3])
    for b in range(4, bands):
        moments = moments + parts[b]
    moments = moments[:, 0 : cpad.shape[1]]
    summed = jnp.zeros(rho_ref.shape, jnp.float32)
    for s in range(2):
        term = jnp.dot(moments, cpad[s], precision=PRECISE, preferred_element_type=jnp.float32)
        summed = jnp.where(kind == s, term, summed)
    ham_ref[...] = jnp.where(live, summed + coul, 0.0)


def apply_kernel(ham_ref, proj_ref, out_ham_ref, out_ref):
    out_ham_ref[...] = ham_ref[...]
    square = NI * NI
    row, col = iota((square, square), 0), iota((square, square), 1)
    spread = (lax.rem(row, NI) == lax.rem(col, NI)).astype(jnp.bfloat16)
    same_i = lax.rem(row, NI) == col // NI
    same_a = row // NI == col // NI
    for t in range(ham_ref.shape[0] // NI):
        block = ham_ref[t * NI : (t + 1) * NI, :]
        tall = jnp.broadcast_to(block[:, None, :], (NI, NI, square)).reshape(square, square)
        high, low = split(jnp.where(same_i, tall, 0.0))
        d_high = jnp.where(same_a, mm(high, spread), 0.0).astype(jnp.bfloat16)
        d_low = jnp.where(same_a, mm(low, spread), 0.0).astype(jnp.bfloat16)
        p_high, p_low = split(proj_ref[t * square : (t + 1) * square, :])
        out_ref[t * square : (t + 1) * square, :] = mm(d_high, p_high) + (
            mm(d_high, p_low) + mm(d_low, p_high)
        )


def local(
    density, hartree, box_root, species, atom_count, shape_functions, coupling, coulomb, rho_ij, projections
):
    f32 = jnp.float32
    wx, wy, depth = density.shape
    bands = lax.axis_size("band")
    slots = box_root.shape[1]
    kinds, comps, cells = shape_functions.shape
    vmem = pl.BlockSpec(memory_space=pltpu.VMEM)
    smem = pl.BlockSpec(memory_space=pltpu.SMEM)
    species_row = species.reshape(1, slots)

    face = lambda *s: pltpu.VMEM(s, f32)
    potential, atoms = pl.pallas_call(
        grid_kernel,
        name="grid_kernel",
        out_shape=(
            jax.ShapeDtypeStruct((wx, wy, depth), f32),
            jax.ShapeDtypeStruct((2, 8, 256), jnp.int32),
        ),
        in_specs=[vmem, vmem, vmem, vmem, smem],
        out_specs=(vmem, vmem),
        scratch_shapes=[
            face(wx + 2, wy + 16, depth), face(wx + 2, wy, depth), face(wx, wy + 16, depth),
            face(wx, wy, depth), face(wx, wy, depth),
            face(2, wy, depth), face(2, wx, depth), face(wy, depth),
            face(2, wy, depth), face(2, wx, depth), face(2, wy, depth),
            face(2, wy, depth), face(2, wx, depth), face(wy, depth),
            face(2, wy, depth), face(2, wx, depth), face(2, wy, depth),
            pltpu.VMEM((8, 128), jnp.int32), pltpu.VMEM((3, 8, 128), jnp.int32),
            pltpu.SemaphoreType.DMA((15,)), pltpu.SemaphoreType.DMA((15,)),
        ],
        compiler_params=pltpu.CompilerParams(
            collective_id=0, has_side_effects=True, vmem_limit_bytes=VMEM_LIMIT
        ),
    )(density, hartree, box_root, species_row, atom_count)

    turned = shape_functions.reshape(kinds, comps, BOX * BOX, BOX)
    turned = turned.transpose(0, 1, 3, 2).reshape(kinds, comps * BOX, BOX * BOX)
    rounded = lax.reduce_precision(turned, 8, 7)
    high, low = rounded.astype(jnp.bfloat16), (turned - rounded).astype(jnp.bfloat16)
    lanes = GROUP * BOX
    potential, partial = pl.pallas_call(
        functools.partial(moment_kernel, depth * bands),
        name="moment_kernel",
        out_shape=(
            jax.ShapeDtypeStruct((wx, wy, depth), f32),
            jax.ShapeDtypeStruct((4, slots, 128), f32),
        ),
        in_specs=[smem, vmem, vmem, vmem],
        out_specs=(vmem, vmem),
        scratch_shapes=[
            face((wx + 2 * PAD) * (wy + 2 * PAD), depth),
            face(BOX * BOX, lanes), face(128, lanes), face(8 + 4 * slots, 128),
        ],
        compiler_params=pltpu.CompilerParams(vmem_limit_bytes=VMEM_LIMIT),
    )(atoms, potential, high, low)

    ham = pl.pallas_call(
        block_kernel,
        name="block_kernel",
        out_shape=jax.ShapeDtypeStruct(rho_ij.shape, f32),
        in_specs=[vmem, vmem, smem, vmem, vmem, vmem],
        out_specs=vmem,
        scratch_shapes=[
            face(3, slots, 128), face(bands, slots, 128), face(slots, 128), face(2, 32, NI * NI),
            pltpu.SemaphoreType.DMA((2 + bands,)), pltpu.SemaphoreType.DMA((2 + bands,)),
        ],
        compiler_params=pltpu.CompilerParams(
            collective_id=1, has_side_effects=True, vmem_limit_bytes=VMEM_LIMIT
        ),
    )(partial, species_row, atom_count, coupling, coulomb, rho_ij)

    width = projections.shape[2]
    ham, applied = pl.pallas_call(
        apply_kernel,
        name="apply_kernel",
        out_shape=(
            jax.ShapeDtypeStruct(rho_ij.shape, f32),
            jax.ShapeDtypeStruct((slots * NI, width), f32),
        ),
        in_specs=[vmem, vmem],
        out_specs=(vmem, vmem),
        compiler_params=pltpu.CompilerParams(vmem_limit_bytes=VMEM_LIMIT),
    )(ham, projections.reshape(slots * NI, width))
    return potential, ham, applied.reshape(slots, NI, width)


def solution(mesh):
    in_specs = (
        P("dx", "dyz", "band"),
        P("dx", "dyz", "band"),
        P(None, ("dx", "dyz")),
        P(("dx", "dyz")),
        P(("dx", "dyz")),
        P(),
        P(),
        P(),
        P(("dx", "dyz"), None),
        P(("dx", "dyz"), None, "band"),
    )
    out_specs = (P("dx", "dyz", "band"), P(("dx", "dyz"), None), P(("dx", "dyz"), None, "band"))
    return jax.shard_map(local, mesh=mesh, in_specs=in_specs, out_specs=out_specs, check_vma=False)
```

time: 254 us -> 48.2 us (0.19)
  matrix products: 133 us -> 0 us
  local copies, waits for them, and re-layouts: 55.6 us -> 13.3 us
  Pallas kernels: 0 us -> 33.4 us
  starting transfers between devices: 20.1 us -> 0 us
  waiting for transfers between devices: 18.4 us -> 0 us
  other arithmetic: 14 us -> 0.12 us
  blocking collectives: 10.4 us -> 0 us
    dot_general x21 -> x0, matrix products: 133 us -> none  [the longest x4 59 us: block_moments(): along_x = jnp.einsum('xjak,aix->ijak', along_y, select_x, precision=PRECISE)]
    pallas_call x0 -> x4, Pallas kernels: none -> 33.4 us  [the longest x1 16.3 us: local(): pl.pallas_call(grid_kernel, name='grid_kernel', out_shape=(jax.ShapeDtype...]
    reshape x7 -> x1, local copies, waits for them, and re-layouts: 30.1 us -> 5.3 us  [local(): turned = shape_functions.reshape(kinds, comps, BOX * BOX, BOX)]
    ppermute x14 -> x0, starting transfers between devices: 20.1 us -> none  [the longest x6 10.5 us: padded_2(): after = lax.ppermute(leading, axis, down)]
    ppermute x14 -> x0, waiting for transfers between devices: 18.4 us -> none  [the longest x6 9.63 us: padded_2(): before = lax.ppermute(last, axis, up)]
    psum x1 -> x0, blocking collectives: 10.4 us -> none  [local(): moments = lax.psum(partial_value, 'band')]
    slice x10 -> x0, local copies, waits for them, and re-layouts: 9.47 us -> none  [the longest x3 4.89 us: padded_2(): last = lax.slice_in_dim(array, length - width, length, axis=dim)]
    ppermute x4 -> x0, local copies, waits for them, and re-layouts: 7.15 us -> none  [the longest x2 3.93 us: padded_2(): before = lax.ppermute(last, axis, up)]
  transfers between devices with their start and end apart: 14 -> 0, of which waited for: 8 -> 0; matrix products, arithmetic and copies ran while one was open for 9% -> 0% of each run, Pallas kernels for 0% -> 0%
where the time goes in v1:
time: 48.2 us
  Pallas kernels  33.4 us (69%)
  local copies, waits for them, and re-layouts  13.3 us (28%)
  between operations  1.37 us (3%)
    pallas_call x1, Pallas kernels, local(): pl.pallas_call(grid_kernel, name='grid_kernel', out_shape=(jax.ShapeDtype...  16.3 us
    pallas_call x1, Pallas kernels, local(): pl.pallas_call(block_kernel, name='block_kernel', out_shape=jax.ShapeDtyp...  9.4 us
    pallas_call x1, Pallas kernels, local(): pl.pallas_call(functools.partial(moment_kernel, depth * bands), name='mom...  5.7 us
    reshape x1, local copies, waits for them, and re-layouts, local(): turned = shape_functions.reshape(kinds, comps, BOX * BOX, BOX)  5.3 us
    transpose x1, local copies, waits for them, and re-layouts, local(): turned = turned.transpose(0, 1, 3, 2).reshape(kinds, comps * BOX, BOX * BOX)  4.67 us
    unnamed x19, local copies, waits for them, and re-layouts  3.35 us
    pallas_call x1, Pallas kernels, local(): pl.pallas_call(apply_kernel, name='apply_kernel', out_shape=(jax.ShapeDty...  2.03 us

profile of v1, /device:TPU:0, one launch (start us, length us, event | category | flops | bytes accessed | tf_op | source)
XLA Modules:
  0.0 48.2 jit_solution(16428419923002270217)
XLA Ops:
  1.3 0.0 copy-start.2
  1.3 1.0 %copy-done.2 = f32[32,24,128]{2,1,0:T(8,128)S(1)} copy-done((f32[32,24,128]{2,1,0:T(8,128)S(1)}, f32[32,24,128]{2,1,0:T(8,128)}, u32[]{:S(2)}) %copy-start.2) | copy-done | bytes 393240
  2.3 0.0 copy-start.3
  2.3 1.0 %copy-done.3 = f32[32,24,128]{2,1,0:T(8,128)S(1)} copy-done((f32[32,24,128]{2,1,0:T(8,128)S(1)}, f32[32,24,128]{2,1,0:T(8,128)}, u32[]{:S(2)}) %copy-start.3) | copy-done | bytes 393240
  3.3 0.0 copy-start.5
  3.3 0.7 %copy-done.5 = s32[3,64]{1,0:T(4,128)S(1)} copy-done((s32[3,64]{1,0:T(4,128)S(1)}, s32[3,64]{1,0:T(4,128)}, u32[]{:S(2)}) %copy-start.5) | copy-done | bytes 792
  4.0 0.0 copy-start.6
  4.0 0.7 %copy-done.6 = s32[64]{0:T(128)S(1)} copy-done((s32[64]{0:T(128)S(1)}, s32[64]{0:T(128)}, u32[]{:S(2)}) %copy-start.6) | copy-done | bytes 280
  4.6 16.3 %grid_kernel.1 = (f32[32,24,128]{2,1,0:T(8,128)S(1)}, s32[2,8,256]{2,1,0:T(8,128)S(1)}) custom-call(f32[32,24,128]{2,1,0:T(8,128)S(1)} %copy-done.2, f32[32,24,128]{2,1,0:T(8,128)S(1)} %copy-done.3, s32[3,64]{1,0:T(4,128)S(1)} %copy-done.5, s32[1,64]{1,0:T(1,128)S(1)} %bitcast.10, s32[1]{0:T(128)S(6)} %copy.17.count_ref), custom_call_target="tpu_custom_call" | custom-call | tf_op jit(solution)/shard_map/grid_kernel/pallas_call | solution.py:389
  20.9 5.3 %reshape.22 = f32[2,25,256,16]{3,2,0,1:T(8,128)} reshape(f32[2,25,4096]{2,0,1:T(2,128)} %param.15) | data formatting | bytes 1638400 | tf_op jit(solution)/shard_map/reshape | solution.py:413
  26.2 0.0 copy-start.1
  26.2 0.0 copy-start.4
  26.2 0.0 copy-start.7
  26.2 0.0 copy-start
  26.2 4.7 %copy.15 = f32[2,25,16,256]{3,2,1,0:T(8,128)S(1)} copy(f32[2,25,16,256]{2,3,0,1:T(8,128)} %bitcast.12) | data formatting | bytes 1638400 | tf_op jit(solution)/shard_map/transpose | solution.py:414
  30.9 0.1 fusion
  31.0 5.7 %moment_kernel.1 = (f32[32,24,128]{2,1,0:T(8,128)}, f32[4,64,128]{2,1,0:T(8,128)S(1)}) custom-call(s32[2,8,256]{2,1,0:T(8,128)S(1)} %get-tuple-element.9.list_ref, f32[32,24,128]{2,1,0:T(8,128)S(1)} %get-tuple-element.10.pot_ref, bf16[2,400,256]{2,1,0:T(8,128)(2,1)S(1)} %get-tuple-element.16.high_ref, bf16[2,400,256]{2,1,0:T(8,128)(2,1)S(1)} %get-tuple-element.15.low_ref), custom_call_target="tpu_custom_call" | custom-call | tf_op jit(solution)/shard_map/moment_kernel/pallas_call | solution.py:418
  36.7 0.0 copy-done.8
  36.7 0.0 copy-done.1
  36.8 0.0 copy-done.4
  36.8 0.0 copy-done.7
  36.8 9.4 %block_kernel.1.ham_ref = f32[64,256]{1,0:T(8,128)S(1)} custom-call(f32[4,64,128]{2,1,0:T(8,128)S(1)} %get-tuple-element.12.part_ref, s32[1,64]{1,0:T(1,128)S(1)} %bitcast.11, s32[1]{0:T(128)S(6)} %copy.17.count_ref, f32[2,25,256]{2,1,0:T(8,128)S(1)} %copy.16.coupling_ref, f32[2,256,256]{2,1,0:T(8,128)S(1)} %copy-done.1, f32[64,256]{1,0:T(8,128)S(1)} %copy-done.4), custom_call_target="tpu_custom_call" | custom-call | tf_op jit(solution)/shard_map/block_kernel/pallas_call | solution.py:434
  46.2 0.0 copy-done
  46.2 2.0 %apply_kernel.1 = (f32[64,256]{1,0:T(8,128)}, f32[1024,128]{1,0:T(8,128)}) custom-call(f32[64,256]{1,0:T(8,128)S(1)} %block_kernel.1.ham_ref, f32[1024,128]{1,0:T(8,128)S(1)} %bitcast.9), custom_call_target="tpu_custom_call" | custom-call | tf_op jit(solution)/shard_map/apply_kernel/pallas_call | solution.py:450
  (2 shorter events, 0.0 us)
Async XLA Ops:
  1.3 1.0 %copy-start.2 = (f32[32,24,128]{2,1,0:T(8,128)S(1)}, f32[32,24,128]{2,1,0:T(8,128)}, u32[]{:S(2)}) copy-start(f32[32,24,128]{2,1,0:T(8,128)} %dens_ref.1) | copy-start | bytes 1179652
  2.3 1.0 %copy-start.3 = (f32[32,24,128]{2,1,0:T(8,128)S(1)}, f32[32,24,128]{2,1,0:T(8,128)}, u32[]{:S(2)}) copy-start(f32[32,24,128]{2,1,0:T(8,128)} %hart_ref.1) | copy-start | bytes 1179652
  3.3 0.7 %copy-start.5 = (s32[3,64]{1,0:T(4,128)S(1)}, s32[3,64]{1,0:T(4,128)}, u32[]{:S(2)}) copy-start(s32[3,64]{1,0:T(4,128)} %root_ref.1) | copy-start | bytes 2308
  4.0 0.7 %copy-start.6 = (s32[64]{0:T(128)S(1)}, s32[64]{0:T(128)}, u32[]{:S(2)}) copy-start(s32[64]{0:T(128)} %param.13) | copy-start | bytes 772
  26.2 10.5 %copy-start.8 = (f32[2,25,256]{2,0,1:T(2,128)S(1)}, f32[2,25,256]{2,0,1:T(2,128)}, u32[]{:S(2)}) copy-start(f32[2,25,256]{2,0,1:T(2,128)} %param.16) | copy-start | bytes 153604
  26.2 10.5 %copy-start.1 = (f32[2,256,256]{2,1,0:T(8,128)S(1)}, f32[2,256,256]{2,1,0:T(8,128)}, u32[]{:S(2)}) copy-start(f32[2,256,256]{2,1,0:T(8,128)} %coulomb_ref.1) | copy-start | bytes 1572868
  26.2 10.5 %copy-start.4 = (f32[64,256]{1,0:T(8,128)S(1)}, f32[64,256]{1,0:T(8,128)}, u32[]{:S(2)}) copy-start(f32[64,256]{1,0:T(8,128)} %rho_ref.1) | copy-start | bytes 196612
  26.2 10.6 %copy-start.7 = (s32[64]{0:T(128)S(1)}, s32[64]{0:T(128)}, u32[]{:S(2)}) copy-start(s32[64]{0:T(128)} %param.13) | copy-start | bytes 772
  26.2 20.0 %copy-start = (f32[64,16,128]{2,1,0:T(8,128)S(1)}, f32[64,16,128]{2,1,0:T(8,128)}, u32[]{:S(2)}) copy-start(f32[64,16,128]{2,1,0:T(8,128)} %param.19) | copy-start | bytes 1572868

commit v2 on v1

--- a/solution.py
+++ b/solution.py
@@ -20,7 +20,7 @@
 PREF = -0.75 * (3.0 / math.pi) ** (1.0 / 3.0)
 RED = 4.0 * (3.0 * math.pi**2) ** (2.0 / 3.0)
 MESH = pl.DeviceIdType.MESH
-VMEM_LIMIT = 48 * 1024 * 1024
+VMEM_LIMIT = 56 * 1024 * 1024
 
 
 def iota(shape, dim):
@@ -66,15 +66,51 @@
     )
 
 
+def turn_shapes(shape_ref, turned, high_ref, low_ref, s):
+    comps, cells = shape_ref.shape[1:]
+    lane, sub = iota((8, 128), 1) // BOX, iota((8, 128), 0)
+    wraps = [(lane // bit) % 2 == 1 for bit in (1, 2, 4)]
+    octets = (comps + 7) // 8
+    row, col = iota((cells // BOX, cells // BOX), 0), iota((cells // BOX, cells // BOX), 1)
+    order = (row // 8 == col // 8) & (lax.rem(row + col, 8) == 0)
+    order = order.astype(jnp.bfloat16)
+    for o in range(octets):
+        for t in range(cells // 128):
+            here = slice(t * 128, (t + 1) * 128)
+            if 8 * o + 8 <= comps:
+                tile = shape_ref[s, 8 * o : 8 * o + 8, here]
+            else:
+                tile = jnp.broadcast_to(shape_ref[s, 8 * o : 8 * o + 1, here], (8, 128))
+            tile = pltpu.roll(tile, 0, 1, stride=BOX, stride_axis=0)
+            for bit, wrap in zip((1, 2, 4), wraps):
+                tile = jnp.where(wrap, pltpu.roll(tile, 8 - bit, 0), tile)
+            tile = pltpu.roll(tile, 0, 1, stride=BOX, stride_axis=0)
+            turned[t * 8 : (t + 1) * 8, :] = tile
+        block = turned[...].T
+        rows = min(128, (comps - 8 * o) * BOX)
+        high, low = split(block[0:rows, :])
+        high_ref[s, o * 128 : o * 128 + rows, :] = mm(high, order).astype(jnp.bfloat16)
+        low_ref[s, o * 128 : o * 128 + rows, :] = mm(low, order).astype(jnp.bfloat16)
+
+
 def grid_kernel(
-    dens_ref, hart_ref, root_ref, species_ref, count_ref,
-    pot_ref, list_ref,
+    dens_hbm, hart_hbm, shape_hbm, root_ref, species_ref, count_ref,
+    pot_ref, list_ref, high_ref, low_ref,
+    dens_ref, hart_ref, shape_ref, turned, local_sems,
     dpad, fxp, fyp, fz, slope_n_ref,
     send_x, send_y, send_z, recv_x, recv_y, recv_z,
     gsend_x, gsend_y, gsend_z, grecv_x, grecv_y, grecv_z,
     plan_send, plan_recv, send_sems, recv_sems,
 ):
     wx, wy, depth = dens_ref.shape
+    loads = [
+        pltpu.make_async_copy(src, dst, local_sems.at[i])
+        for i, (src, dst) in enumerate(
+            ((dens_hbm, dens_ref), (shape_hbm, shape_ref), (hart_hbm, hart_ref))
+        )
+    ]
+    for load in loads:
+        load.start()
     up_x, down_x = {"dx": shifted("dx", 1)}, {"dx": shifted("dx", -1)}
     up_y, down_y = {"dyz": shifted("dyz", 1)}, {"dyz": shifted("dyz", -1)}
     up_z, down_z = {"band": shifted("band", 1)}, {"band": shifted("band", -1)}
@@ -90,6 +126,7 @@
         copy.start()
         return copy
 
+    loads[0].wait()
     send_x[0] = dens_ref[wx - 1]
     send_x[1] = dens_ref[0]
     send_y[0] = dens_ref[:, wy - 1, :]
@@ -117,6 +154,8 @@
         remote(plan_send, plan_recv.at[2], 8, up_xy),
     ]
     dpad[1 : wx + 1, 8 : wy + 8, :] = dens_ref[...]
+    loads[1].wait()
+    turn_shapes(shape_ref, turned, high_ref, low_ref, 0)
     for copy in first:
         copy.wait()
     dpad[0, 8 : wy + 8, :] = recv_x[0]
@@ -137,13 +176,13 @@
         sigma = gx * gx + gy * gy + gz * gz
         log_n = jnp.log(here)
         cube = jnp.exp(log_n * (1.0 / 3.0))
-        inv = 1.0 / (here * cube)
-        r = sigma * inv * inv * (1.0 / RED)
-        u = 1.0 / (1.0 + (MU_COEF / KAPPA) * r)
-        slope_r = MU_COEF * u * u
-        slope_s = (PREF / RED) * slope_r * inv
-        enhance = 1.0 + KAPPA - KAPPA * u
-        slope_n_ref[x] = (4.0 / 3.0 * PREF) * cube * (enhance - 2.0 * r * slope_r)
+        power = here * cube
+        scaled = RED * power * power
+        summed = scaled + (MU_COEF / KAPPA) * sigma
+        both = 1.0 / (power * summed)
+        u = scaled * power * both
+        slope_s = (PREF / RED * MU_COEF) * u * u * (summed * both)
+        slope_n_ref[x] = (4.0 / 3.0 * PREF) * cube * (1.0 + KAPPA - KAPPA * u * (3.0 - 2.0 * u))
         fxp[x + 1] = slope_s * gx
         fyp[x, 8 : wy + 8, :] = slope_s * gy
         fz[x] = slope_s * gz
@@ -188,26 +227,35 @@
         meets &= (z < depth) | (z > depth_all - BOX)
         rows = (x + PAD) * (wy + 2 * PAD) + (y + PAD)
         dest = 8 + c * slots + slot
-        columns.append((meets, rows, z, dest, plan[3:4, :]))
-    meets, rows, z, dest, kind = [jnp.concatenate([c[f].astype(jnp.int32) for c in columns], 1) for f in range(5)]
-    wide = 4 * 128
+        columns.append([v.astype(jnp.int32) for v in (meets, rows, z, dest, plan[3:4, :])])
+    left = iota((1, 128), 1) < slots
+    merged = []
+    for f in range(5):
+        halves = [
+            jnp.where(left, columns[c][f], pltpu.roll(columns[c + 1][f], slots, 1)) for c in (0, 2)
+        ]
+        merged.append(jnp.concatenate(halves, 1))
+    meets, rows, z, dest, kind = merged
+    wide = 256
     upper = (iota((wide, wide), 0) <= iota((wide, wide), 1)).astype(jnp.bfloat16)
     row8 = iota((8, wide), 0)
     picked = jnp.where((meets == 1) & (kind == row8), 1.0, 0.0)
     order = mm(picked.astype(jnp.bfloat16), upper)
+    place = iota((wide, wide), 0).astype(jnp.float32) + 1.0
     fields = jnp.where(row8 == 0, rows, jnp.where(row8 == 1, z, jnp.where(row8 == 2, dest, 0)))
-    fields = fields.astype(jnp.float32)
+    f_high, f_low = split(fields.astype(jnp.float32))
+    across = (((1,), (1,)), ((), ()))
     for s in range(2):
         total = jnp.sum(picked[s : s + 1, :], axis=1, keepdims=True)
-        place = iota((256, wide), 0).astype(jnp.float32) + 1.0
-        onehot = jnp.where((order[s : s + 1, :] == place) & (picked[s : s + 1, :] > 0.5), 1.0, 0.0)
-        got = lax.dot_general(
-            fields, onehot, (((1,), (1,)), ((), ())), precision=PRECISE,
-            preferred_element_type=jnp.float32,
-        )
-        got = jnp.where(iota((8, 256), 0) == 3, total, got)
+        spot = jnp.where(picked[s : s + 1, :] > 0.5, order[s : s + 1, :], 0.0)
+        onehot = (spot == place).astype(jnp.bfloat16)
+        got = lax.dot_general(f_high, onehot, across, preferred_element_type=jnp.float32)
+        got = got + lax.dot_general(f_low, onehot, across, preferred_element_type=jnp.float32)
+        got = jnp.where(row8 == 3, total, got)
         list_ref[s] = (got + 0.5).astype(jnp.int32)
-
+    turn_shapes(shape_ref, turned, high_ref, low_ref, 1)
+
+    loads[2].wait()
     for copy in second:
         copy.wait()
     fxp[0] = grecv_x[0]
@@ -248,6 +296,7 @@
     sums[...] = jnp.zeros_like(sums)
     folded[...] = jnp.zeros_like(folded)
     lanes = GROUP * BOX
+    per_tile = 128 // BOX
     lane = iota((BOX, 128), 1)
     adder = (iota((GROUP, lanes), 0) == iota((GROUP, lanes), 1) // BOX).astype(jnp.float32)
     keep = lax.rem(iota((BOX, lanes), 1), BOX) == iota((BOX, lanes), 0)
@@ -256,25 +305,31 @@
         total = list_ref[s, 3, 0]
 
         def one_group(g, carry, s=s, total=total):
-            gathered[...] = jnp.zeros_like(gathered)
-            for q in range(GROUP):
-                p = g * GROUP + q
-
-                @pl.when(p < total)
-                def _(q=q, p=p):
-                    row = list_ref[s, 0, p]
-                    z = list_ref[s, 1, p]
-                    left = (q * BOX) % 128
-                    tile = q * BOX // 128 * 128
-                    shift = lax.rem(left + depth_all - z, depth)
-                    cell = z + lane - left
-                    cell = jnp.where(cell >= depth_all, cell - depth_all, cell)
-                    mine = (lane >= left) & (lane < left + BOX) & (cell < depth)
+            for tile in range(lanes // 128):
+                first = g * GROUP + tile * per_tile
+                across = slice(tile * 128, (tile + 1) * 128)
+
+                @pl.when(first < total)
+                def _(first=first, across=across):
+                    plan = []
+                    for q in range(per_tile):
+                        left = q * BOX
+                        z = list_ref[s, 1, first + q]
+                        shift = lax.rem(left + depth_all - z, depth)
+                        cell = z + lane - left
+                        cell = jnp.where(cell >= depth_all, cell - depth_all, cell)
+                        mine = (lane >= left) & (lane < left + BOX) & (cell < depth)
+                        plan.append((list_ref[s, 0, first + q], shift, mine))
                     for i in range(BOX):
-                        piece = padded[pl.ds(row + i * rows_y, BOX), :]
-                        piece = pltpu.roll(piece, shift, 1)
-                        spot = (slice(i * BOX, (i + 1) * BOX), slice(tile, tile + 128))
-                        gathered[spot] = jnp.where(mine, piece, gathered[spot])
+                        made = jnp.zeros((BOX, 128), jnp.float32)
+                        for row, shift, mine in plan:
+                            piece = padded[pl.ds(row + i * rows_y, BOX), :]
+                            made = jnp.where(mine, pltpu.roll(piece, shift, 1), made)
+                        gathered[i * BOX : (i + 1) * BOX, across] = made
+
+                @pl.when(first >= total)
+                def _(across=across):
+                    gathered[:, across] = jnp.zeros((BOX * BOX, 128), jnp.float32)
 
             g_high, g_low = split(gathered[...])
             product = mm(high_ref[s], g_high) + (mm(high_ref[s], g_low) + mm(low_ref[s], g_high))
@@ -382,20 +437,26 @@
     slots = box_root.shape[1]
     kinds, comps, cells = shape_functions.shape
     vmem = pl.BlockSpec(memory_space=pltpu.VMEM)
+    anywhere = pl.BlockSpec(memory_space=pl.ANY)
     smem = pl.BlockSpec(memory_space=pltpu.SMEM)
     species_row = species.reshape(1, slots)
 
     face = lambda *s: pltpu.VMEM(s, f32)
-    potential, atoms = pl.pallas_call(
+    turned_shape = jax.ShapeDtypeStruct((kinds, comps * BOX, BOX * BOX), jnp.bfloat16)
+    potential, atoms, high, low = pl.pallas_call(
         grid_kernel,
         name="grid_kernel",
         out_shape=(
             jax.ShapeDtypeStruct((wx, wy, depth), f32),
             jax.ShapeDtypeStruct((2, 8, 256), jnp.int32),
+            turned_shape,
+            turned_shape,
         ),
-        in_specs=[vmem, vmem, vmem, vmem, smem],
-        out_specs=(vmem, vmem),
+        in_specs=[anywhere, anywhere, anywhere, vmem, vmem, smem],
+        out_specs=(vmem,) * 4,
         scratch_shapes=[
+            face(wx, wy, depth), face(wx, wy, depth), face(kinds, comps, cells),
+            face(BOX * BOX, 128), pltpu.SemaphoreType.DMA((3,)),
             face(wx + 2, wy + 16, depth), face(wx + 2, wy, depth), face(wx, wy + 16, depth),
             face(wx, wy, depth), face(wx, wy, depth),
             face(2, wy, depth), face(2, wx, depth), face(wy, depth),
@@ -408,12 +469,8 @@
         compiler_params=pltpu.CompilerParams(
             collective_id=0, has_side_effects=True, vmem_limit_bytes=VMEM_LIMIT
         ),
-    )(density, hartree, box_root, species_row, atom_count)
-
-    turned = shape_functions.reshape(kinds, comps, BOX * BOX, BOX)
-    turned = turned.transpose(0, 1, 3, 2).reshape(kinds, comps * BOX, BOX * BOX)
-    rounded = lax.reduce_precision(turned, 8, 7)
-    high, low = rounded.astype(jnp.bfloat16), (turned - rounded).astype(jnp.bfloat16)
+    )(density, hartree, shape_functions, box_root, species_row, atom_count)
+
     lanes = GROUP * BOX
     potential, partial = pl.pallas_call(
         functools.partial(moment_kernel, depth * bands),

time: 48.2 us -> 43 us (0.89); the launches traced: 48.2 us -> 42.3 us
  local copies, waits for them, and re-layouts: 13.3 us -> 3.24 us
  Pallas kernels: 33.4 us -> 37.8 us
    reshape x1 -> x0, local copies, waits for them, and re-layouts: 5.3 us -> none  [local(): turned = shape_functions.reshape(kinds, comps, BOX * BOX, BOX)]
    transpose x1 -> x0, local copies, waits for them, and re-layouts: 4.67 us -> none  [local(): turned = turned.transpose(0, 1, 3, 2).reshape(kinds, comps * BOX, BOX * BOX)]
    pallas_call x1, Pallas kernels: 16.3 us -> 18.9 us  [local(): pl.pallas_call(grid_kernel, name='grid_kernel', out_shape=(jax.ShapeDtype...]
    pallas_call x1, Pallas kernels: 9.4 us -> 10.6 us  [local(): pl.pallas_call(block_kernel, name='block_kernel', out_shape=jax.ShapeDtyp...]
    pallas_call x1, Pallas kernels: 2.03 us -> 3.11 us  [local(): pl.pallas_call(apply_kernel, name='apply_kernel', out_shape=(jax.ShapeDty...]
    pallas_call x1, Pallas kernels: 5.7 us -> 5.14 us  [local(): pl.pallas_call(functools.partial(moment_kernel, depth * bands), name='mom...]
    unnamed x19 -> x4, local copies, waits for them, and re-layouts: 3.35 us -> 3.24 us
where the time goes in v2:
time: 43 us; the launch traced here: 42.3 us
  Pallas kernels  37.8 us (88%)
  local copies, waits for them, and re-layouts  3.24 us (8%)
  between operations  1.3 us (3%)
    pallas_call x1, Pallas kernels, local(): pl.pallas_call(grid_kernel, name='grid_kernel', out_shape=(jax.ShapeDtype...  18.9 us
    pallas_call x1, Pallas kernels, local(): pl.pallas_call(block_kernel, name='block_kernel', out_shape=jax.ShapeDtyp...  10.6 us
    pallas_call x1, Pallas kernels, local(): pl.pallas_call(functools.partial(moment_kernel, depth * bands), name='mom...  5.14 us
    unnamed x4, local copies, waits for them, and re-layouts  3.24 us
    pallas_call x1, Pallas kernels, local(): pl.pallas_call(apply_kernel, name='apply_kernel', out_shape=(jax.ShapeDty...  3.11 us

profile of v2, /device:TPU:0, one launch (start us, length us, event | category | flops | bytes accessed | tf_op | source)
XLA Modules:
  0.0 42.3 jit_solution(5935627758032283156)
XLA Ops:
  1.3 2.6 %copy.13.shape_hbm = f32[2,25,4096]{2,1,0:T(8,128)} copy(f32[2,25,4096]{2,0,1:T(2,128)} %param.15) | data formatting | bytes 1638400 | tf_op args[5]
  3.9 18.9 %grid_kernel.1 = (f32[32,24,128]{2,1,0:T(8,128)}, s32[2,8,256]{2,1,0:T(8,128)}, bf16[2,400,256]{2,1,0:T(8,128)(2,1)}, bf16[2,400,256]{2,1,0:T(8,128)(2,1)}) custom-call(f32[32,24,128]{2,1,0:T(8,128)} %dens_hbm.1, f32[32,24,128]{2,1,0:T(8,128)} %hart_hbm.1, f32[2,25,4096]{2,1,0:T(8,128)} %copy.13.shape_hbm, s32[3,64]{1,0:T(4,128)} %root_ref.1, ...), custom_call_target="tpu_custom_call" | custom-call | tf_op jit(solution)/shard_map/grid_kernel/pallas_call | solution.py:446
  22.8 0.0 copy-start
  22.8 5.1 %moment_kernel.1 = (f32[32,24,128]{2,1,0:T(8,128)}, f32[4,64,128]{2,1,0:T(8,128)}) custom-call(s32[2,8,256]{2,1,0:T(8,128)} %get-tuple-element.11.list_ref, f32[32,24,128]{2,1,0:T(8,128)} %get-tuple-element.12.pot_ref, bf16[2,400,256]{2,1,0:T(8,128)(2,1)} %get-tuple-element.13.high_ref, bf16[2,400,256]{2,1,0:T(8,128)(2,1)} %get-tuple-element.14.low_ref), custom_call_target="tpu_custom_call" | custom-call | tf_op jit(solution)/shard_map/moment_kernel/pallas_call | solution.py:475
  28.0 0.0 copy-done
  28.0 0.6 %copy.14.coupling_ref = f32[2,25,256]{2,1,0:T(8,128)} copy(f32[2,25,256]{2,0,1:T(2,128)S(1)} %copy-done) | data formatting | bytes 102400 | tf_op args[6]
  28.6 10.6 %block_kernel.1.ham_ref = f32[64,256]{1,0:T(8,128)} custom-call(f32[4,64,128]{2,1,0:T(8,128)} %get-tuple-element.16.part_ref, s32[1,64]{1,0:T(1,128)} %bitcast.5, s32[1]{0:T(128)S(6)} %copy.15.count_ref, f32[2,25,256]{2,1,0:T(8,128)} %copy.14.coupling_ref, f32[2,256,256]{2,1,0:T(8,128)} %coulomb_ref.1, f32[64,256]{1,0:T(8,128)} %rho_ref.1), custom_call_target="tpu_custom_call" | custom-call | tf_op jit(solution)/shard_map/block_kernel/pallas_call | solution.py:491
  39.2 3.1 %apply_kernel.1 = (f32[64,256]{1,0:T(8,128)}, f32[1024,128]{1,0:T(8,128)}) custom-call(f32[64,256]{1,0:T(8,128)} %block_kernel.1.ham_ref, f32[1024,128]{1,0:T(8,128)} %bitcast.3), custom_call_target="tpu_custom_call" | custom-call | tf_op jit(solution)/shard_map/apply_kernel/pallas_call | solution.py:507
Async XLA Ops:
  22.8 5.2 %copy-start = (f32[2,25,256]{2,0,1:T(2,128)S(1)}, f32[2,25,256]{2,0,1:T(2,128)}, u32[]{:S(2)}) copy-start(f32[2,25,256]{2,0,1:T(2,128)} %param.16) | copy-start | bytes 153604

commit v3 on v2

--- a/solution.py
+++ b/solution.py
@@ -11,6 +11,7 @@
 BOX = 16
 NI = 16
 GROUP = 16
+LANES = 32
 PAD = 16
 GRID_H = 0.15
 KAPPA = 0.804
@@ -20,7 +21,7 @@
 PREF = -0.75 * (3.0 / math.pi) ** (1.0 / 3.0)
 RED = 4.0 * (3.0 * math.pi**2) ** (2.0 / 3.0)
 MESH = pl.DeviceIdType.MESH
-VMEM_LIMIT = 56 * 1024 * 1024
+VMEM_LIMIT = 20 * 1024 * 1024
 
 
 def iota(shape, dim):
@@ -106,7 +107,12 @@
     loads = [
         pltpu.make_async_copy(src, dst, local_sems.at[i])
         for i, (src, dst) in enumerate(
-            ((dens_hbm, dens_ref), (shape_hbm, shape_ref), (hart_hbm, hart_ref))
+            (
+                (dens_hbm, dens_ref),
+                (shape_hbm.at[:, 0, :], shape_ref.at[0]),
+                (shape_hbm.at[:, 1, :], shape_ref.at[1]),
+                (hart_hbm, hart_ref),
+            )
         )
     ]
     for load in loads:
@@ -253,9 +259,10 @@
         got = got + lax.dot_general(f_low, onehot, across, preferred_element_type=jnp.float32)
         got = jnp.where(row8 == 3, total, got)
         list_ref[s] = (got + 0.5).astype(jnp.int32)
+    loads[2].wait()
     turn_shapes(shape_ref, turned, high_ref, low_ref, 1)
 
-    loads[2].wait()
+    loads[3].wait()
     for copy in second:
         copy.wait()
     fxp[0] = grecv_x[0]
@@ -283,12 +290,13 @@
 
 
 def moment_kernel(
-    depth_all, list_ref, pot_ref, high_ref, low_ref, out_pot_ref, out_ref, padded, gathered, folded, sums
+    depth_all, list_ref, pot_ref, high_ref, low_ref, out_pot_ref, out_ref, padded, gathered, folded, sums, sem
 ):
     wx, wy, depth = pot_ref.shape
     rows_y = wy + 2 * PAD
     comps = high_ref.shape[1] // BOX
-    out_pot_ref[...] = pot_ref[...]
+    store = pltpu.make_async_copy(pot_ref, out_pot_ref, sem)
+    store.start()
     padded[...] = jnp.zeros_like(padded)
     for x in range(wx):
         start = (x + PAD) * rows_y + PAD
@@ -345,9 +353,14 @@
             return carry
 
         lax.fori_loop(0, (total + GROUP - 1) // GROUP, one_group, 0)
-    slots = out_ref.shape[1]
+    slots = (sums.shape[0] - 8) // 4
     for c in range(4):
-        out_ref[c] = sums[8 + c * slots : 8 + (c + 1) * slots, :]
+        held = jnp.zeros(out_ref.shape[1:], jnp.float32)
+        for r in range(slots // GROUP):
+            start = 8 + c * slots + r * GROUP
+            held = held + pltpu.roll(sums[start : start + GROUP, :], r * LANES, 1)
+        out_ref[c] = held
+    store.wait()
 
 
 def block_kernel(
@@ -356,7 +369,7 @@
 ):
     bands = lax.axis_size("band")
     me = lax.axis_index("band")
-    slots = part_ref.shape[1]
+    slots = rho_ref.shape[0]
     up_x, down_x = {"dx": shifted("dx", 1)}, {"dx": shifted("dx", -1)}
     up_y, down_y = {"dyz": shifted("dyz", 1)}, {"dyz": shifted("dyz", -1)}
     up_xy = {"dx": shifted("dx", 1), "dyz": shifted("dyz", 1)}
@@ -380,11 +393,11 @@
     kind = jnp.sum(jnp.where(eye, species_ref[...], 0), axis=1, keepdims=True)
     live = iota((slots, 1), 0) < count_ref[0]
     cpad[...] = jnp.zeros_like(cpad)
-    comps = coupling_ref.shape[1]
+    comps = coupling_ref.shape[0]
     rho_high, rho_low = split(rho_ref[...])
     coul = jnp.zeros(rho_ref.shape, jnp.float32)
     for s in range(2):
-        cpad[s, 0:comps, :] = coupling_ref[s]
+        cpad[s, 0:comps, :] = coupling_ref[:, s, :]
         c_high, c_low = split(coulomb_ref[s])
         term = mm(rho_high, c_high) + (mm(rho_high, c_low) + mm(rho_low, c_high))
         coul = jnp.where(kind == s, 2.0 * term, coul)
@@ -401,7 +414,8 @@
     moments = (parts[0] + parts[1]) + (parts[2] + parts[3])
     for b in range(4, bands):
         moments = moments + parts[b]
-    moments = moments[:, 0 : cpad.shape[1]]
+    rows = [pltpu.roll(moments, (128 - r * LANES) % 128, 1) for r in range(slots // GROUP)]
+    moments = jnp.concatenate(rows, 0)[:, 0:LANES]
     summed = jnp.zeros(rho_ref.shape, jnp.float32)
     for s in range(2):
         term = jnp.dot(moments, cpad[s], precision=PRECISE, preferred_element_type=jnp.float32)
@@ -409,8 +423,9 @@
     ham_ref[...] = jnp.where(live, summed + coul, 0.0)
 
 
-def apply_kernel(ham_ref, proj_ref, out_ham_ref, out_ref):
+def apply_kernel(ham_ref, proj_ref, out_ham_ref, out_hbm, out_ref, sems):
     out_ham_ref[...] = ham_ref[...]
+    stores = []
     square = NI * NI
     row, col = iota((square, square), 0), iota((square, square), 1)
     spread = (lax.rem(row, NI) == lax.rem(col, NI)).astype(jnp.bfloat16)
@@ -426,6 +441,11 @@
         out_ref[t * square : (t + 1) * square, :] = mm(d_high, p_high) + (
             mm(d_high, p_low) + mm(d_low, p_high)
         )
+        rows = pl.ds(t * square, square)
+        stores.append(pltpu.make_async_copy(out_ref.at[rows], out_hbm.at[rows], sems.at[t]))
+        stores[-1].start()
+    for store in stores:
+        store.wait()
 
 
 def local(
@@ -437,7 +457,7 @@
     slots = box_root.shape[1]
     kinds, comps, cells = shape_functions.shape
     vmem = pl.BlockSpec(memory_space=pltpu.VMEM)
-    anywhere = pl.BlockSpec(memory_space=pl.ANY)
+    hbm = pl.BlockSpec(memory_space=pltpu.HBM)
     smem = pl.BlockSpec(memory_space=pltpu.SMEM)
     species_row = species.reshape(1, slots)
 
@@ -452,11 +472,11 @@
             turned_shape,
             turned_shape,
         ),
-        in_specs=[anywhere, anywhere, anywhere, vmem, vmem, smem],
+        in_specs=[hbm, hbm, hbm, vmem, vmem, smem],
         out_specs=(vmem,) * 4,
         scratch_shapes=[
             face(wx, wy, depth), face(wx, wy, depth), face(kinds, comps, cells),
-            face(BOX * BOX, 128), pltpu.SemaphoreType.DMA((3,)),
+            face(BOX * BOX, 128), pltpu.SemaphoreType.DMA((4,)),
             face(wx + 2, wy + 16, depth), face(wx + 2, wy, depth), face(wx, wy + 16, depth),
             face(wx, wy, depth), face(wx, wy, depth),
             face(2, wy, depth), face(2, wx, depth), face(wy, depth),
@@ -467,9 +487,9 @@
             pltpu.SemaphoreType.DMA((15,)), pltpu.SemaphoreType.DMA((15,)),
         ],
         compiler_params=pltpu.CompilerParams(
-            collective_id=0, has_side_effects=True, vmem_limit_bytes=VMEM_LIMIT
+            collective_id=0, has_side_effects=True, vmem_limit_bytes=56 * 1024 * 1024
         ),
-    )(density, hartree, shape_functions, box_root, species_row, atom_count)
+    )(density, hartree, shape_functions.transpose(1, 0, 2), box_root, species_row, atom_count)
 
     lanes = GROUP * BOX
     potential, partial = pl.pallas_call(
@@ -477,13 +497,14 @@
         name="moment_kernel",
         out_shape=(
             jax.ShapeDtypeStruct((wx, wy, depth), f32),
-            jax.ShapeDtypeStruct((4, slots, 128), f32),
+            jax.ShapeDtypeStruct((4, GROUP, 128), f32),
         ),
         in_specs=[smem, vmem, vmem, vmem],
-        out_specs=(vmem, vmem),
+        out_specs=(hbm, vmem),
         scratch_shapes=[
             face((wx + 2 * PAD) * (wy + 2 * PAD), depth),
             face(BOX * BOX, lanes), face(128, lanes), face(8 + 4 * slots, 128),
+            pltpu.SemaphoreType.DMA,
         ],
         compiler_params=pltpu.CompilerParams(vmem_limit_bytes=VMEM_LIMIT),
     )(atoms, potential, high, low)
@@ -495,13 +516,13 @@
         in_specs=[vmem, vmem, smem, vmem, vmem, vmem],
         out_specs=vmem,
         scratch_shapes=[
-            face(3, slots, 128), face(bands, slots, 128), face(slots, 128), face(2, 32, NI * NI),
+            face(3, GROUP, 128), face(bands, GROUP, 128), face(GROUP, 128), face(2, LANES, NI * NI),
             pltpu.SemaphoreType.DMA((2 + bands,)), pltpu.SemaphoreType.DMA((2 + bands,)),
         ],
         compiler_params=pltpu.CompilerParams(
             collective_id=1, has_side_effects=True, vmem_limit_bytes=VMEM_LIMIT
         ),
-    )(partial, species_row, atom_count, coupling, coulomb, rho_ij)
+    )(partial, species_row, atom_count, coupling.transpose(1, 0, 2), coulomb, rho_ij)
 
     width = projections.shape[2]
     ham, applied = pl.pallas_call(
@@ -512,7 +533,8 @@
             jax.ShapeDtypeStruct((slots * NI, width), f32),
         ),
         in_specs=[vmem, vmem],
-        out_specs=(vmem, vmem),
+        out_specs=(vmem, hbm),
+        scratch_shapes=[face(slots * NI, width), pltpu.SemaphoreType.DMA((slots // NI,))],
         compiler_params=pltpu.CompilerParams(vmem_limit_bytes=VMEM_LIMIT),
     )(ham, projections.reshape(slots * NI, width))
     return potential, ham, applied.reshape(slots, NI, width)

time: 43 us -> 39.4 us (0.916); the launches traced: 42.3 us -> 39.2 us
  Pallas kernels: 37.8 us -> 34.1 us
  local copies, waits for them, and re-layouts: 3.24 us -> 3.73 us
    pallas_call x1, Pallas kernels: 10.6 us -> 7.54 us  [local(): pl.pallas_call(block_kernel, name='block_kernel', out_shape=jax.ShapeDtyp...]
    pallas_call x1, Pallas kernels: 3.11 us -> 2.55 us  [local(): pl.pallas_call(apply_kernel, name='apply_kernel', out_shape=(jax.ShapeDty...]
    unnamed x4 -> x18, local copies, waits for them, and re-layouts: 3.24 us -> 3.73 us
where the time goes in v3:
time: 39.4 us; the launch traced here: 39.2 us
  Pallas kernels  34.1 us (87%)
  local copies, waits for them, and re-layouts  3.73 us (9%)
  between operations  1.37 us (3%)
    pallas_call x1, Pallas kernels, local(): pl.pallas_call(grid_kernel, name='grid_kernel', out_shape=(jax.ShapeDtype...  18.9 us
    pallas_call x1, Pallas kernels, local(): pl.pallas_call(block_kernel, name='block_kernel', out_shape=jax.ShapeDtyp...  7.54 us
    pallas_call x1, Pallas kernels, local(): pl.pallas_call(functools.partial(moment_kernel, depth * bands), name='mom...  5.09 us
    unnamed x18, local copies, waits for them, and re-layouts  3.73 us
    pallas_call x1, Pallas kernels, local(): pl.pallas_call(apply_kernel, name='apply_kernel', out_shape=(jax.ShapeDty...  2.55 us

profile of v3, /device:TPU:0, one launch (start us, length us, event | category | flops | bytes accessed | tf_op | source)
XLA Modules:
  0.0 39.2 jit_solution(4084746179349247173)
XLA Ops:
  1.3 18.9 %grid_kernel.1 = (f32[32,24,128]{2,1,0:T(8,128)}, s32[2,8,256]{2,1,0:T(8,128)}, bf16[2,400,256]{2,1,0:T(8,128)(2,1)}, bf16[2,400,256]{2,1,0:T(8,128)(2,1)}) custom-call(f32[32,24,128]{2,1,0:T(8,128)} %dens_hbm.1, f32[32,24,128]{2,1,0:T(8,128)} %hart_hbm.1, f32[25,2,4096]{2,1,0:T(2,128)} %bitcast.9, s32[3,64]{1,0:T(4,128)} %root_ref.1, s32[1,64]{1,0:T(1,128)} %bitcast.7, ...), custom_call_target="tpu_custom_call" | custom-call | tf_op jit(solution)/shard_map/grid_kernel/pallas_call | solution.py:466
  20.2 0.0 copy-start.2
  20.2 1.0 %copy-done.2 = bf16[2,400,256]{2,1,0:T(8,128)(2,1)S(1)} copy-done((bf16[2,400,256]{2,1,0:T(8,128)(2,1)S(1)}, bf16[2,400,256]{2,1,0:T(8,128)(2,1)}, u32[]{:S(2)}) %copy-start.2) | copy-done | bytes 409624
  21.2 0.0 copy-start.3
  21.2 1.0 %copy-done.3 = bf16[2,400,256]{2,1,0:T(8,128)(2,1)S(1)} copy-done((bf16[2,400,256]{2,1,0:T(8,128)(2,1)S(1)}, bf16[2,400,256]{2,1,0:T(8,128)(2,1)}, u32[]{:S(2)}) %copy-start.3) | copy-done | bytes 409624
  22.2 0.0 copy-start.4
  22.2 1.0 %copy-done.4 = f32[32,24,128]{2,1,0:T(8,128)S(1)} copy-done((f32[32,24,128]{2,1,0:T(8,128)S(1)}, f32[32,24,128]{2,1,0:T(8,128)}, u32[]{:S(2)}) %copy-start.4) | copy-done | bytes 393240
  23.2 0.0 copy-start.7
  23.2 0.7 %copy-done.7 = s32[2,8,256]{2,1,0:T(8,128)S(1)} copy-done((s32[2,8,256]{2,1,0:T(8,128)S(1)}, s32[2,8,256]{2,1,0:T(8,128)}, u32[]{:S(2)}) %copy-start.7) | copy-done | bytes 16408
  23.9 0.0 copy-start.1
  23.9 0.0 copy-start.5
  23.9 0.0 copy-start.6
  23.9 0.0 copy-start.8
  23.9 5.1 %moment_kernel.1 = (f32[32,24,128]{2,1,0:T(8,128)}, f32[4,16,128]{2,1,0:T(8,128)S(1)}) custom-call(s32[2,8,256]{2,1,0:T(8,128)S(1)} %copy-done.7, f32[32,24,128]{2,1,0:T(8,128)S(1)} %copy-done.4, bf16[2,400,256]{2,1,0:T(8,128)(2,1)S(1)} %copy-done.2, bf16[2,400,256]{2,1,0:T(8,128)(2,1)S(1)} %copy-done.3), custom_call_target="tpu_custom_call" | custom-call | tf_op jit(solution)/shard_map/moment_kernel/pallas_call | solution.py:495
  29.0 0.0 copy-start
  29.0 0.0 copy-done.1
  29.0 0.0 copy-done.5
  29.1 0.0 copy-done.6
  29.1 0.0 copy-done.8
  29.1 7.5 %block_kernel.1.ham_ref = f32[64,256]{1,0:T(8,128)S(1)} custom-call(f32[4,16,128]{2,1,0:T(8,128)S(1)} %get-tuple-element.16.part_ref, s32[1,64]{1,0:T(1,128)S(1)} %bitcast.8, s32[1]{0:T(128)S(6)} %copy.13.count_ref, f32[25,2,256]{2,1,0:T(2,128)S(1)} %bitcast.6, f32[2,256,256]{2,1,0:T(8,128)S(1)} %copy-done.1, f32[64,256]{1,0:T(8,128)S(1)} %copy-done.5), custom_call_target="tpu_custom_call" | custom-call | tf_op jit(solution)/shard_map/block_kernel/pallas_call | solution.py:512
  36.6 0.0 copy-done
  36.6 2.6 %apply_kernel.1 = (f32[64,256]{1,0:T(8,128)}, f32[1024,128]{1,0:T(8,128)}) custom-call(f32[64,256]{1,0:T(8,128)S(1)} %block_kernel.1.ham_ref, f32[1024,128]{1,0:T(8,128)S(1)} %bitcast.5), custom_call_target="tpu_custom_call" | custom-call | tf_op jit(solution)/shard_map/apply_kernel/pallas_call | solution.py:528
Async XLA Ops:
  20.2 1.0 %copy-start.2 = (bf16[2,400,256]{2,1,0:T(8,128)(2,1)S(1)}, bf16[2,400,256]{2,1,0:T(8,128)(2,1)}, u32[]{:S(2)}) copy-start(bf16[2,400,256]{2,1,0:T(8,128)(2,1)} %get-tuple-element.13.high_ref) | copy-start | bytes 1228804
  21.2 1.0 %copy-start.3 = (bf16[2,400,256]{2,1,0:T(8,128)(2,1)S(1)}, bf16[2,400,256]{2,1,0:T(8,128)(2,1)}, u32[]{:S(2)}) copy-start(bf16[2,400,256]{2,1,0:T(8,128)(2,1)} %get-tuple-element.14.low_ref) | copy-start | bytes 1228804
  22.2 1.0 %copy-start.4 = (f32[32,24,128]{2,1,0:T(8,128)S(1)}, f32[32,24,128]{2,1,0:T(8,128)}, u32[]{:S(2)}) copy-start(f32[32,24,128]{2,1,0:T(8,128)} %get-tuple-element.12.pot_ref) | copy-start | bytes 1179652
  23.2 0.7 %copy-start.7 = (s32[2,8,256]{2,1,0:T(8,128)S(1)}, s32[2,8,256]{2,1,0:T(8,128)}, u32[]{:S(2)}) copy-start(s32[2,8,256]{2,1,0:T(8,128)} %get-tuple-element.11.list_ref) | copy-start | bytes 49156
  23.9 5.1 %copy-start.1 = (f32[2,256,256]{2,1,0:T(8,128)S(1)}, f32[2,256,256]{2,1,0:T(8,128)}, u32[]{:S(2)}) copy-start(f32[2,256,256]{2,1,0:T(8,128)} %coulomb_ref.1) | copy-start | bytes 1572868
  23.9 5.1 %copy-start.5 = (f32[64,256]{1,0:T(8,128)S(1)}, f32[64,256]{1,0:T(8,128)}, u32[]{:S(2)}) copy-start(f32[64,256]{1,0:T(8,128)} %rho_ref.1) | copy-start | bytes 196612
  23.9 5.1 %copy-start.6 = (f32[2,25,256]{2,0,1:T(2,128)S(1)}, f32[2,25,256]{2,0,1:T(2,128)}, u32[]{:S(2)}) copy-start(f32[2,25,256]{2,0,1:T(2,128)} %param.16) | copy-start | bytes 153604
  23.9 5.1 %copy-start.8 = (s32[64]{0:T(128)S(1)}, s32[64]{0:T(128)}, u32[]{:S(2)}) copy-start(s32[64]{0:T(128)} %param.13) | copy-start | bytes 772
  29.0 7.6 %copy-start = (f32[64,16,128]{2,1,0:T(8,128)S(1)}, f32[64,16,128]{2,1,0:T(8,128)}, u32[]{:S(2)}) copy-start(f32[64,16,128]{2,1,0:T(8,128)} %param.19) | copy-start | bytes 1572868

commit v4 on v3

--- a/solution.py
+++ b/solution.py
@@ -21,7 +21,7 @@
 PREF = -0.75 * (3.0 / math.pi) ** (1.0 / 3.0)
 RED = 4.0 * (3.0 * math.pi**2) ** (2.0 / 3.0)
 MESH = pl.DeviceIdType.MESH
-VMEM_LIMIT = 20 * 1024 * 1024
+VMEM_LIMIT = 56 * 1024 * 1024
 
 
 def iota(shape, dim):
@@ -290,19 +290,31 @@
 
 
 def moment_kernel(
-    depth_all, list_ref, pot_ref, high_ref, low_ref, out_pot_ref, out_ref, padded, gathered, folded, sums, sem
+    depth_all, list_ref, pot_hbm, high_hbm, low_hbm, out_pot_ref, out_ref,
+    pot_ref, high_ref, low_ref, padded, gathered, folded, sums, load_sems, sem,
 ):
+    loads = [
+        pltpu.make_async_copy(src, dst, load_sems.at[i])
+        for i, (src, dst) in enumerate(
+            ((pot_hbm, pot_ref), (high_hbm, high_ref), (low_hbm, low_ref))
+        )
+    ]
+    for load in loads:
+        load.start()
     wx, wy, depth = pot_ref.shape
     rows_y = wy + 2 * PAD
     comps = high_ref.shape[1] // BOX
+    padded[...] = jnp.zeros_like(padded)
+    sums[...] = jnp.zeros_like(sums)
+    folded[...] = jnp.zeros_like(folded)
+    loads[0].wait()
     store = pltpu.make_async_copy(pot_ref, out_pot_ref, sem)
     store.start()
-    padded[...] = jnp.zeros_like(padded)
     for x in range(wx):
         start = (x + PAD) * rows_y + PAD
         padded[start : start + wy, :] = pot_ref[x]
-    sums[...] = jnp.zeros_like(sums)
-    folded[...] = jnp.zeros_like(folded)
+    loads[1].wait()
+    loads[2].wait()
     lanes = GROUP * BOX
     per_tile = 128 // BOX
     lane = iota((BOX, 128), 1)
@@ -364,8 +376,8 @@
 
 
 def block_kernel(
-    part_ref, species_ref, count_ref, coupling_ref, coulomb_ref, rho_ref, ham_ref,
-    around, parts, total_ref, cpad, send_sems, recv_sems,
+    part_ref, species_ref, count_ref, coupling_ref, coulomb_hbm, rho_hbm, ham_ref,
+    coulomb_ref, rho_ref, load_sems, around, parts, total_ref, cpad, send_sems, recv_sems,
 ):
     bands = lax.axis_size("band")
     me = lax.axis_index("band")
@@ -375,6 +387,12 @@
     up_xy = {"dx": shifted("dx", 1), "dyz": shifted("dyz", 1)}
     down_xy = {"dx": shifted("dx", -1), "dyz": shifted("dyz", -1)}
     others = [{"band": shifted("band", t)} for t in range(1, bands)]
+    loads = [
+        pltpu.make_async_copy(coulomb_hbm, coulomb_ref, load_sems.at[0]),
+        pltpu.make_async_copy(rho_hbm, rho_ref, load_sems.at[1]),
+    ]
+    for load in loads:
+        load.start()
     enter([up_x, down_x, up_y, down_y, up_xy, down_xy] + others)
 
     def remote(src, dst, sem, device):
@@ -394,6 +412,8 @@
     live = iota((slots, 1), 0) < count_ref[0]
     cpad[...] = jnp.zeros_like(cpad)
     comps = coupling_ref.shape[0]
+    for load in loads:
+        load.wait()
     rho_high, rho_low = split(rho_ref[...])
     coul = jnp.zeros(rho_ref.shape, jnp.float32)
     for s in range(2):
@@ -423,7 +443,12 @@
     ham_ref[...] = jnp.where(live, summed + coul, 0.0)
 
 
-def apply_kernel(ham_ref, proj_ref, out_ham_ref, out_hbm, out_ref, sems):
+def apply_kernel(ham_ref, proj_hbm, out_ham_ref, out_hbm, proj_ref, out_ref, load_sems, sems):
+    loads = []
+    for t in range(ham_ref.shape[0] // NI):
+        rows = pl.ds(t * NI * NI, NI * NI)
+        loads.append(pltpu.make_async_copy(proj_hbm.at[rows], proj_ref.at[rows], load_sems.at[t]))
+        loads[-1].start()
     out_ham_ref[...] = ham_ref[...]
     stores = []
     square = NI * NI
@@ -437,6 +462,7 @@
         high, low = split(jnp.where(same_i, tall, 0.0))
         d_high = jnp.where(same_a, mm(high, spread), 0.0).astype(jnp.bfloat16)
         d_low = jnp.where(same_a, mm(low, spread), 0.0).astype(jnp.bfloat16)
+        loads[t].wait()
         p_high, p_low = split(proj_ref[t * square : (t + 1) * square, :])
         out_ref[t * square : (t + 1) * square, :] = mm(d_high, p_high) + (
             mm(d_high, p_low) + mm(d_low, p_high)
@@ -499,12 +525,14 @@
             jax.ShapeDtypeStruct((wx, wy, depth), f32),
             jax.ShapeDtypeStruct((4, GROUP, 128), f32),
         ),
-        in_specs=[smem, vmem, vmem, vmem],
+        in_specs=[smem, hbm, hbm, hbm],
         out_specs=(hbm, vmem),
         scratch_shapes=[
+            face(wx, wy, depth),
+            pltpu.VMEM(turned_shape.shape, jnp.bfloat16), pltpu.VMEM(turned_shape.shape, jnp.bfloat16),
             face((wx + 2 * PAD) * (wy + 2 * PAD), depth),
             face(BOX * BOX, lanes), face(128, lanes), face(8 + 4 * slots, 128),
-            pltpu.SemaphoreType.DMA,
+            pltpu.SemaphoreType.DMA((3,)), pltpu.SemaphoreType.DMA,
         ],
         compiler_params=pltpu.CompilerParams(vmem_limit_bytes=VMEM_LIMIT),
     )(atoms, potential, high, low)
@@ -513,9 +541,10 @@
         block_kernel,
         name="block_kernel",
         out_shape=jax.ShapeDtypeStruct(rho_ij.shape, f32),
-        in_specs=[vmem, vmem, smem, vmem, vmem, vmem],
+        in_specs=[vmem, vmem, smem, vmem, hbm, hbm],
         out_specs=vmem,
         scratch_shapes=[
+            face(*coulomb.shape), face(*rho_ij.shape), pltpu.SemaphoreType.DMA((2,)),
             face(3, GROUP, 128), face(bands, GROUP, 128), face(GROUP, 128), face(2, LANES, NI * NI),
             pltpu.SemaphoreType.DMA((2 + bands,)), pltpu.SemaphoreType.DMA((2 + bands,)),
         ],
@@ -532,9 +561,12 @@
             jax.ShapeDtypeStruct(rho_ij.shape, f32),
             jax.ShapeDtypeStruct((slots * NI, width), f32),
         ),
-        in_specs=[vmem, vmem],
+        in_specs=[vmem, hbm],
         out_specs=(vmem, hbm),
-        scratch_shapes=[face(slots * NI, width), pltpu.SemaphoreType.DMA((slots // NI,))],
+        scratch_shapes=[
+            face(slots * NI, width), face(slots * NI, width),
+            pltpu.SemaphoreType.DMA((slots // NI,)), pltpu.SemaphoreType.DMA((slots // NI,)),
+        ],
         compiler_params=pltpu.CompilerParams(vmem_limit_bytes=VMEM_LIMIT),
     )(ham, projections.reshape(slots * NI, width))
     return potential, ham, applied.reshape(slots, NI, width)

time: 39.4 us -> 40.3 us (1.023)
  Pallas kernels: 34.1 us -> 38.5 us
  local copies, waits for them, and re-layouts: 3.73 us -> 0 us
    unnamed x18 -> x0, local copies, waits for them, and re-layouts: 3.73 us -> none
    pallas_call x1, Pallas kernels: 7.54 us -> 9.68 us  [local(): pl.pallas_call(block_kernel, name='block_kernel', out_shape=jax.ShapeDtyp...]
    pallas_call x1, Pallas kernels: 2.55 us -> 4.46 us  [local(): pl.pallas_call(apply_kernel, name='apply_kernel', out_shape=(jax.ShapeDty...]
    pallas_call x1, Pallas kernels: 5.09 us -> 5.49 us  [local(): pl.pallas_call(functools.partial(moment_kernel, depth * bands), name='mom...]
where the time goes in v4:
time: 40.3 us; the launch traced here: 39.8 us
  Pallas kernels  38.5 us (96%)
  between operations  1.3 us (3%)
    pallas_call x1, Pallas kernels, local(): pl.pallas_call(grid_kernel, name='grid_kernel', out_shape=(jax.ShapeDtype...  18.9 us
    pallas_call x1, Pallas kernels, local(): pl.pallas_call(block_kernel, name='block_kernel', out_shape=jax.ShapeDtyp...  9.68 us
    pallas_call x1, Pallas kernels, local(): pl.pallas_call(functools.partial(moment_kernel, depth * bands), name='mom...  5.49 us
    pallas_call x1, Pallas kernels, local(): pl.pallas_call(apply_kernel, name='apply_kernel', out_shape=(jax.ShapeDty...  4.46 us

profile of v4, /device:TPU:0, one launch (start us, length us, event | category | flops | bytes accessed | tf_op | source)
XLA Modules:
  0.0 39.8 jit_solution(3712536447770215212)
XLA Ops:
  1.3 18.9 %grid_kernel.1 = (f32[32,24,128]{2,1,0:T(8,128)}, s32[2,8,256]{2,1,0:T(8,128)}, bf16[2,400,256]{2,1,0:T(8,128)(2,1)}, bf16[2,400,256]{2,1,0:T(8,128)(2,1)}) custom-call(f32[32,24,128]{2,1,0:T(8,128)} %dens_hbm.1, f32[32,24,128]{2,1,0:T(8,128)} %hart_hbm.1, f32[25,2,4096]{2,1,0:T(2,128)} %bitcast.5, s32[3,64]{1,0:T(4,128)} %root_ref.1, s32[1,64]{1,0:T(1,128)} %bitcast.8, ...), custom_call_target="tpu_custom_call" | custom-call | tf_op jit(solution)/shard_map/grid_kernel/pallas_call | solution.py:492
  20.2 5.5 %moment_kernel.1 = (f32[32,24,128]{2,1,0:T(8,128)}, f32[4,16,128]{2,1,0:T(8,128)}) custom-call(s32[2,8,256]{2,1,0:T(8,128)} %get-tuple-element.11.list_ref, f32[32,24,128]{2,1,0:T(8,128)} %get-tuple-element.12.pot_hbm, bf16[2,400,256]{2,1,0:T(8,128)(2,1)} %get-tuple-element.13.high_hbm, bf16[2,400,256]{2,1,0:T(8,128)(2,1)} %get-tuple-element.14.low_hbm), custom_call_target="tpu_custom_call" | custom-call | tf_op jit(solution)/shard_map/moment_kernel/pallas_call | solution.py:521
  25.7 9.7 %block_kernel.1.ham_ref = f32[64,256]{1,0:T(8,128)} custom-call(f32[4,16,128]{2,1,0:T(8,128)} %get-tuple-element.16.part_ref, s32[1,64]{1,0:T(1,128)} %bitcast.9, s32[1]{0:T(128)S(6)} %copy.13.count_ref, f32[25,2,256]{2,1,0:T(2,128)} %bitcast.7, f32[2,256,256]{2,1,0:T(8,128)} %coulomb_hbm.1, f32[64,256]{1,0:T(8,128)} %rho_hbm.1), custom_call_target="tpu_custom_call" | custom-call | tf_op jit(solution)/shard_map/block_kernel/pallas_call | solution.py:540
  35.4 4.5 %apply_kernel.1 = (f32[64,256]{1,0:T(8,128)}, f32[1024,128]{1,0:T(8,128)}) custom-call(f32[64,256]{1,0:T(8,128)} %block_kernel.1.ham_ref, f32[1024,128]{1,0:T(8,128)} %bitcast.6), custom_call_target="tpu_custom_call" | custom-call | tf_op jit(solution)/shard_map/apply_kernel/pallas_call | solution.py:557
